TPU v7x, 32 devices: a whole 2x2x4 slice. The times are simulated.
32 devices in a mesh: groups: 2 (over x), view: 16 (over z, y, core).
Axes of the slice: x: 2, y: 2, z: 4, core: 2. Of those that a mesh axis runs over, the one named last changes fastest.
Arguments:
- ref_features: bfloat16 [256, 32, 384], P(('groups', 'view')), parts along dimension 0, may hold values from -6 to 6
- source_tiles: bfloat16 [1024, 2, 32, 384], P(('groups', 'view')), parts along dimension 0, may hold values from -6 to 6
- pair_lists: int32 [32, 4, 4], P(('groups', 'view')), parts along dimension 0, may hold values from -1 to 511, as said below
- view_counts: int32 [32], P(('groups', 'view')), parts along dimension 0, may hold values from 3 to 4, as said below
- disparities: int32 [16, 4], P('groups'), parts along dimension 0, may hold values from -48 to 48
- conv_first: bfloat16 [3, 3, 8, 3, 32], replicated, may hold values from -0.21875 to 0.21875
- bias_first: float32 [8], replicated, may hold values from -3 to 3
- conv_second: bfloat16 [16, 3, 3, 3, 8], replicated, may hold values from -0.4375 to 0.4375
- bias_second: float32 [16], replicated, may hold values from -3 to 3
Outputs:
- cost_features: float32 [8, 64, 16, 192], P('groups', 'view'), parts along dimension 0
There are 2 independent parts, one for each index of `groups`. A program takes and returns all parts, laid end to end along the dimension named above; an argument that names none is the same for every part. Nothing has to cross between parts.
Inputs may be any that keep to these rules, and one draw needn't show every extreme that they name: pair_lists[v, s, b] is the tile holding rows 2b and 2b + 1 of source s of strip v; it is -1 exactly when s >= view_counts[v]; tile t lies on device t // 32 of the view axis; no strip takes more than 2 tiles from one device, and some strip takes exactly 2 from some device. `view_counts`: some strip uses 3 sources and some uses 4.
All inputs are finite; a program needn't handle non-finite values.
Results may differ from a plain program's by a relative error of at most 0.0028.
Values may be sent and summed in bfloat16 or wider, within the bound.
No kernel may reach another device: no remote copies, remote signals or barrier semaphores. Data moves between devices by JAX's collectives and lax.ppermute only.
A program may use at most 128 MiB of HBM per device.

v0:
```python
import functools

import numpy as np

import jax
import jax.numpy as jnp
from jax import lax
from jax.experimental import pallas as pl
from jax.experimental.pallas import tpu as pltpu
from jax.sharding import PartitionSpec as P

SHIFT = 48
CAP = 2
LANES = 128
CHUNK = 64
VMEM_LIMIT = 10 * 1024 * 1024


def swapped(x, axis, parity):
    count = lax.axis_size(axis)
    pairs = [(i, i + 1) for i in range(parity, count - 1, 2)]
    return lax.ppermute(x, axis, pairs + [(j, i) for i, j in pairs])


def request_places(pair_lists, tiles_dev):
    owners, ranks, tiles = [], [], []
    for s in range(pair_lists.shape[1]):
        for b in range(pair_lists.shape[2]):
            tile = pair_lists[0, s, b]
            whole = jnp.maximum(tile, 0)
            owner = jnp.where(tile >= 0, lax.div(whole, tiles_dev), -1)
            rank = jnp.int32(0)
            for other in owners:
                rank = rank + jnp.where(other == owner, 1, 0)
            owners.append(owner)
            ranks.append(rank)
            tiles.append(lax.rem(whole, tiles_dev))
    return owners, ranks, tiles


def request_kernel(tiles_dev, pair_lists, table):
    n_view = table.shape[0]
    row = lax.broadcasted_iota(jnp.int32, (n_view, LANES), 0) * tiles_dev
    lane = lax.broadcasted_iota(jnp.int32, (n_view, LANES), 1)
    total = jnp.zeros((n_view, LANES), jnp.int32)
    count = jnp.zeros((n_view, LANES), jnp.int32)
    for s in range(pair_lists.shape[1]):
        for b in range(pair_lists.shape[2]):
            tile = pair_lists[0, s : s + 1, b : b + 1] - row
            owned = (tile >= 0) & (tile < tiles_dev)
            total = jnp.where(owned & (lane == count), tile, total)
            count = count + jnp.where(owned, 1, 0)
    total = jnp.where(lane == CAP, lax.broadcasted_iota(jnp.int32, (n_view, LANES), 0), total)
    for d in range(n_view):
        table[d] = total[d : d + 1, : table.shape[2]]


def gather_kernel(distances, n_view, table, tiles, *bundles):
    me = table[0, CAP]
    for k, bundle in zip(distances, bundles):
        at = lax.rem(me + k, n_view) * (CAP + 1)
        for j in range(CAP):
            bundle[j] = tiles[table[0, at + j]]


def collect_kernel(distances, *refs):
    arrived = refs[-1]
    for k, bundle in zip(distances, refs[:-1]):
        for j in range(CAP):
            arrived[k * CAP + j] = bundle[j]


def prepare_kernel(
    n_view,
    tiles_dev,
    edge_rows,
    mid_rows,
    first,
    second,
    bias_first,
    bias_second,
    disparities,
    pair_lists,
    view_counts,
    me,
    kernel_edge,
    kernel_mid,
    two_mid,
    two_edge,
    bias_rows,
    bias_two,
    scalars,
    stacked_mid,
    stacked_edge,
):
    planes, sources = disparities.shape
    owners, ranks, _ = request_places(pair_lists, tiles_dev)
    at = 0
    for p in range(planes):
        for s in range(sources):
            scalars[at] = disparities[p, s]
            at += 1
    for owner, rank in zip(owners, ranks):
        back = lax.rem(me[0] - owner + n_view, n_view)
        scalars[at] = jnp.where(owner >= 0, back * CAP + rank, 0)
        at += 1
    scalars[at] = view_counts[0]
    scalars[at + 1] = me[0]
    scalars[at + 2] = lax.rem(me[0], 2)
    tail = kernel_edge.shape[0] - 8
    lane_at = lax.broadcasted_iota(jnp.int32, (8, LANES), 1)
    numbers = jnp.zeros((8, LANES), jnp.float32)
    for i in range(at + 3):
        numbers = jnp.where(lane_at == i, scalars[i].astype(jnp.float32), numbers)
    kernel_edge[tail:, :] = numbers

    c1, channels = first.shape[3], first.shape[4]
    c2 = second.shape[4]
    rows_n = len(edge_rows) + len(mid_rows)
    half_r = rows_n // 2
    place = {row: i for i, row in enumerate(edge_rows + mid_rows)}
    per_group = LANES // channels
    filler = jnp.zeros((c1, LANES - channels), jnp.float32)
    taps = {}
    for a in range(3):
        for b in range(3):
            for d in range(3):
                tap = jnp.concatenate([first[a, b, d].astype(jnp.float32), filler], axis=1)
                for turn in range(per_group):
                    lane = turn * channels
                    taps[a, b, d, turn] = pltpu.roll(tap, lane, 1) if lane else tap

    def band(a, d, r, group):
        total = jnp.zeros((c1, LANES), jnp.float32)
        for b in range(3):
            at_place = place.get(r - 1 + b, -1)
            if at_place >= 0 and at_place // per_group == group:
                total = total + taps[a, b, d, at_place % per_group]
        return total

    rim = (-1, 0, rows_n - 1, rows_n)
    inner = tuple(range(1, rows_n - 1))
    for kernel, rows, groups in ((kernel_edge, (rim[0],) + rim[2:], 1), (kernel_mid, (0,) + inner, 2)):
        for d in range(3):
            for i, r in enumerate(rows):
                for a in range(3):
                    at = ((a * 3 + d) * len(rows) + i) * c1
                    for group in range(groups):
                        kernel[at : at + c1, group * LANES : (group + 1) * LANES] = band(a, d, r, group)

    def second_row(a, d, r):
        blocks = []
        for g in range(half_r):
            b = -1 if r is None else r - 2 * g + 1
            hit = 0 <= b < 3
            blocks.append(second[a, b, d].astype(jnp.float32) if hit else jnp.zeros((c1, c2), jnp.float32))
        blocks.append(jnp.zeros((c1, LANES - half_r * c2), jnp.float32))
        return jnp.concatenate(blocks, axis=1)

    for two, stacked, rows in ((two_mid, stacked_mid, inner), (two_edge, stacked_edge, rim[:3] + (None,))):
        deep = two.shape[1]
        stacked[...] = jnp.zeros(stacked.shape, jnp.float32)
        for a in range(3):
            for j, d in enumerate((1, 0, 2)):
                for i, r in enumerate(rows):
                    at = j * deep + (a * len(rows) + i) * c1
                    stacked[at : at + c1, :] = second_row(a, d, r)
        outs = half_r * c2
        for j in range(3):
            two[j * outs : (j + 1) * outs, :] = stacked[j * deep : (j + 1) * deep, :].T[:outs].astype(jnp.bfloat16)

    def spread_bias(like, bias):
        index = lax.broadcasted_iota(jnp.int32, like.shape, 0)
        total = jnp.zeros(like.shape, jnp.float32)
        for i in range(bias.shape[0]):
            total = jnp.where(index % bias.shape[0] == i, bias[i], total)
        like[...] = total

    spread_bias(bias_rows, bias_first)
    spread_bias(bias_two, bias_second)


def plane_variance(p, sources, cols, disp, wide, ref_wide, inv):
    chunks = []
    for x0 in range(0, cols, CHUNK):
        ref = ref_wide[0, x0 : x0 + CHUNK, :]
        summed = ref
        squares = ref * ref
        for s in range(sources):
            warped = wide[s, pl.ds(SHIFT + x0 - disp[p * sources + s], CHUNK), :]
            summed = summed + warped
            squares = squares + warped * warped
        chunks.append((squares - summed * summed * inv).astype(jnp.bfloat16))
    return jnp.concatenate(chunks, axis=0)


def view_weights(live):
    total = live.astype(jnp.float32) + jnp.ones((1, LANES), jnp.float32)
    return 1.0 / total, lax.rsqrt(total)


def turned_reference(ref, blocks, picks):
    tile_rows = ref.shape[0] // blocks
    rows = [ref[block * tile_rows + i] for block in picks for i in range(tile_rows)]
    return jnp.concatenate(rows, axis=0).T.astype(jnp.float32)


def clear_bands(wide, cols):
    band = jnp.zeros((SHIFT, LANES), jnp.float32)
    for at in range(wide.shape[0]):
        wide[at, 0:SHIFT, :] = band
        wide[at, SHIFT + cols : 2 * SHIFT + cols, :] = band


def load_tiles(at_slots, live, sources, blocks, picks, scale, scalars, arrived, wide):
    for s in range(sources):
        slab = jnp.concatenate([arrived[scalars[at_slots + s * blocks + block]] for block in picks], axis=0)
        cols = slab.shape[1]
        wide[s, SHIFT : SHIFT + cols, :] = slab.T.astype(jnp.float32) * jnp.where(s < live, scale, 0.0)


def add_plane(q, planes, lhs, weights, sums):
    taps = lax.dot_general(weights, lhs, (((1,), (1,)), ((), ())), preferred_element_type=jnp.float32)
    rows = taps.shape[0] // 3
    slots = sums.shape[0]
    if q + 1 < planes:
        sums[(q + 1) % slots] = taps[:rows]
    if q == 0:
        sums[q % slots] = taps[rows : 2 * rows]
    else:
        sums[q % slots] += taps[rows : 2 * rows]
        sums[(q - 1) % slots] += taps[2 * rows :]


def joined_columns(taps, column):
    rows, cols = column.shape
    left, center, right = taps[:rows], taps[rows : 2 * rows], taps[2 * rows :]
    total = center + jnp.where(column > 0, pltpu.roll(left, 1, 1), 0.0)
    return total + jnp.where(column < cols - 1, pltpu.roll(right, cols - 1, 1), 0.0)


def strided_planes(q, planes, taken, rows, weights, out_w):
    step = taken.shape[1] // 2
    none = jnp.zeros((rows, 2 * step), jnp.bfloat16)
    near = range(2 * q - 1, 2 * q + 2)
    parts = [taken[p * rows : (p + 1) * rows] if 0 <= p < planes else none for p in near]
    rhs = jnp.concatenate(parts, axis=0)
    deep = rhs.shape[0]
    outs = weights.shape[0] // 3
    even = jnp.dot(weights[:outs, :deep], rhs[:, :step], preferred_element_type=jnp.float32)
    odd = jnp.dot(weights[outs:, :deep], rhs[:, step:], preferred_element_type=jnp.float32)
    result = even + pltpu.roll(odd[:outs], 1, 1) + odd[outs:]
    return result[:, :out_w]


def edge_kernel(
    at_slots, at_live, sources, blocks, picks, packed, arrived, ref, var, own, far, near, flags, wide, ref_wide, sums, held, sem
):
    planes, cols, _ = var.shape
    tail = packed.shape[0] - 8
    c1 = tail // 27
    copy = pltpu.make_async_copy(packed.at[pl.ds(tail, 1)], held, sem)
    copy.start()
    weights = packed[:tail].astype(jnp.bfloat16)
    turned = turned_reference(ref, blocks, picks)
    clear_bands(wide, cols)
    copy.wait()
    scalars = [held[0, i].astype(jnp.int32) for i in range(at_live + 3)]
    live = scalars[at_live]
    inv, scale = view_weights(live)
    ref_wide[0] = turned * scale
    load_tiles(at_slots, live, sources, blocks, picks, scale, scalars, arrived, wide)
    odd = scalars[at_live + 2] > 0
    flags[0] = jnp.where(odd, 1.0, 0.0) * jnp.ones((c1, LANES), jnp.float32)
    flags[1] = jnp.where(scalars[at_live + 1] > 0, 1.0, 0.0) * jnp.ones((c1, LANES), jnp.float32)
    column = lax.broadcasted_iota(jnp.int32, (3 * c1, cols), 1)
    empty = jnp.zeros((c1, cols), jnp.float32)

    def finish(p):
        total = joined_columns(sums[p % sums.shape[0]], column)
        own[p] = total[: 2 * c1]
        downward = total[c1:]
        upward = jnp.concatenate([total[:c1], empty], axis=0)
        far[p] = jnp.where(odd, downward, upward).astype(jnp.bfloat16)
        near[p] = jnp.where(odd, upward, downward).astype(jnp.bfloat16)

    values = plane_variance(0, sources, cols, scalars, wide, ref_wide, inv)
    for q in range(planes):
        held_values = values
        if q + 1 < planes:
            values = plane_variance(q + 1, sources, cols, scalars, wide, ref_wide, inv)
        add_plane(q, planes, held_values, weights, sums)
        var[q] = held_values
        if q > 0:
            finish(q - 1)
    finish(planes - 1)


def mid_kernel(
    at_slots,
    at_live,
    sources,
    blocks,
    picks,
    numbers,
    arrived,
    ref,
    edge_var,
    kernel,
    bias_rows,
    kernel_two,
    bias_two,
    out,
    own,
    choices,
    wide,
    ref_wide,
    cost,
    sums,
    scalars,
    sem,
):
    copy = pltpu.make_async_copy(numbers, scalars, sem)
    copy.start()
    planes, cols, _ = edge_var.shape
    inner = cost.shape[0] // planes
    step = choices.shape[1] // 2
    row = lax.broadcasted_iota(jnp.int32, (cols, step), 0)
    target = 2 * lax.broadcasted_iota(jnp.int32, (cols, step), 1)
    for odd in range(2):
        choices[:, odd * step : (odd + 1) * step] = jnp.where(row == target + odd, 1.0, 0.0).astype(jnp.bfloat16)
    turned = turned_reference(ref, blocks, picks)
    clear_bands(wide, cols)
    copy.wait()
    live = scalars[at_live]
    inv, scale = view_weights(live)
    ref_wide[0] = turned * scale
    load_tiles(at_slots, live, sources, blocks, picks, scale, scalars, arrived, wide)
    weights = kernel[...].astype(jnp.bfloat16)
    bias = bias_rows[:inner]
    ready, cols = own.shape[1:]
    column = lax.broadcasted_iota(jnp.int32, (ready + inner, cols), 1)

    def finish(p):
        total = joined_columns(sums[p % sums.shape[0]], column)
        own[p] = total[:ready]
        cost[p * inner : (p + 1) * inner, :] = jnp.maximum(total[ready:] + bias, 0.0).astype(jnp.bfloat16)

    values = plane_variance(0, sources, cols, scalars, wide, ref_wide, inv)
    for q in range(planes):
        held_values = values
        if q + 1 < planes:
            values = plane_variance(q + 1, sources, cols, scalars, wide, ref_wide, inv)
        add_plane(q, planes, jnp.concatenate([edge_var[q], held_values], axis=1), weights, sums)
        if q > 0:
            finish(q - 1)
    finish(planes - 1)
    taken = jnp.dot(cost[...], choices[...], preferred_element_type=jnp.float32).astype(jnp.bfloat16)
    for q in range(planes // 2):
        out[q] = strided_planes(q, planes, taken, inner, kernel_two, out.shape[2]) + bias_two[...]


def end_kernel(far, near, flags, own, own_top, partial, bias_rows, kernel_two, choices, out):
    planes, c1, cols = own_top.shape
    odd = jnp.concatenate([flags[0]] * (cols // LANES), axis=1) > 0.5
    not_top = jnp.concatenate([flags[1]] * (cols // LANES), axis=1)
    empty = jnp.zeros((c1, cols), jnp.float32)
    bias = bias_rows[:c1]
    rows = []
    for p in range(planes):
        lower, upper = far[p].astype(jnp.float32), near[p].astype(jnp.float32)
        before = own[p, :c1] + jnp.where(odd, upper[:c1], lower[:c1])
        top = own_top[p] + jnp.where(odd, upper[c1:], lower[c1:])
        bottom = own[p, c1:] + jnp.where(odd, lower[:c1], upper[:c1])
        rows += [jnp.maximum(before + bias, 0.0) * not_top]
        rows += [jnp.maximum(top + bias, 0.0), jnp.maximum(bottom + bias, 0.0), empty]
    cost = jnp.concatenate(rows, axis=0).astype(jnp.bfloat16)
    taken = jnp.dot(cost, choices[...], preferred_element_type=jnp.float32).astype(jnp.bfloat16)
    for q in range(planes // 2):
        out[q] = partial[q] + strided_planes(q, planes, taken, 4 * c1, kernel_two, out.shape[2])


def on_device(
    ref_features,
    source_tiles,
    pair_lists,
    view_counts,
    disparities,
    conv_first,
    bias_first,
    conv_second,
    bias_second,
):
    n_view = lax.axis_size("view")
    me = lax.axis_index("view").reshape(1)
    rows_n, channels, cols = ref_features.shape
    tiles_dev, tile_rows = source_tiles.shape[0], source_tiles.shape[1]
    sources, blocks = pair_lists.shape[1], pair_lists.shape[2]
    planes = disparities.shape[0]
    slab = tile_rows * channels
    c1, c2 = conv_first.shape[2], conv_second.shape[0]
    half_r, half_p, half_x = rows_n // 2, planes // 2, cols // 2
    smem = pl.BlockSpec(memory_space=pltpu.SMEM)
    vmem = pl.BlockSpec(memory_space=pltpu.VMEM)
    anywhere = pl.BlockSpec(memory_space=pl.ANY)
    params = pltpu.CompilerParams(vmem_limit_bytes=VMEM_LIMIT)
    bf16, f32, i32 = jnp.bfloat16, jnp.float32, jnp.int32
    shape = jax.ShapeDtypeStruct

    table = pl.pallas_call(
        functools.partial(request_kernel, tiles_dev),
        out_shape=shape((n_view, 1, 2 * CAP), i32),
        in_specs=[vmem],
        out_specs=vmem,
        compiler_params=params,
        name="request_table",
    )(pair_lists)
    table = lax.all_to_all(table, "view", split_axis=0, concat_axis=0, tiled=True)
    tiles = source_tiles.reshape(tiles_dev, slab, cols)
    table = table[:, 0, : CAP + 1].reshape(1, n_view * (CAP + 1))
    far_first = sorted(range(1, n_view), key=lambda k: -min(k, n_view - k))
    order = [k for pair in zip(far_first, far_first[::-1]) for k in pair][: len(far_first)]
    distances = order + [0]
    bundles = [None] * n_view
    gathered = pl.pallas_call(
        functools.partial(gather_kernel, distances, n_view),
        out_shape=[shape((CAP, slab, cols), bf16)] * n_view,
        in_specs=[smem, vmem],
        out_specs=[vmem] * n_view,
        compiler_params=params,
        name="requested_tiles",
    )(table, tiles)
    for k, bundle in zip(distances, gathered):
        pairs = [(i, (i + k) % n_view) for i in range(n_view)]
        bundles[k] = lax.ppermute(bundle, "view", pairs) if k else bundle

    at_slots = planes * sources
    at_live = at_slots + sources * blocks
    edge_blocks, mid_blocks = (0, blocks - 1), tuple(range(1, blocks - 1))
    rows_of = lambda picks: [block * tile_rows + i for block in picks for i in range(tile_rows)]
    edge_rows, mid_rows = rows_of(edge_blocks), rows_of(mid_blocks)
    inner = (rows_n - 2) * c1
    mid_deep, edge_deep = (-(-3 * rows // LANES) * LANES for rows in (inner, 4 * c1))
    prepared = pl.pallas_call(
        functools.partial(prepare_kernel, n_view, tiles_dev, edge_rows, mid_rows),
        out_shape=[
            shape((27 * c1 + 8, LANES), f32),
            shape((9 * (inner + c1), 2 * LANES), f32),
            shape((3 * half_r * c2, mid_deep), bf16),
            shape((3 * half_r * c2, edge_deep), bf16),
            shape((inner, cols), f32),
            shape((half_r * c2, half_x), f32),
            shape((LANES,), i32),
        ],
        in_specs=[vmem, vmem] + [smem] * 6,
        out_specs=[vmem] * 6 + [smem],
        scratch_shapes=[pltpu.VMEM((3 * mid_deep, LANES), f32), pltpu.VMEM((3 * edge_deep, LANES), f32)],
        compiler_params=params,
        name="weights_and_scalars",
    )(
        conv_first.transpose(0, 1, 3, 2, 4),
        conv_second.transpose(1, 2, 3, 4, 0),
        bias_first,
        bias_second,
        disparities,
        pair_lists,
        view_counts,
        me,
    )
    kernel_edge, kernel_mid, two_mid, two_edge, bias_rows, bias_two, scalars = prepared
    arrived = pl.pallas_call(
        functools.partial(collect_kernel, distances),
        out_shape=shape((n_view * CAP, slab, cols), bf16),
        in_specs=[vmem] * n_view,
        out_specs=vmem,
        compiler_params=params,
        name="all_tiles",
    )(*[bundles[k] for k in distances])

    band_scratch = [pltpu.VMEM((sources, cols + 2 * SHIFT, LANES), f32), pltpu.VMEM((1, cols, LANES), f32)]
    payload = shape((planes, 2 * c1, cols), bf16)
    col_step = (half_x // LANES + 1) * LANES
    edge_var, own, far, near, flags = pl.pallas_call(
        functools.partial(edge_kernel, at_slots, at_live, sources, blocks, edge_blocks),
        out_shape=[
            shape((planes, cols, LANES), bf16),
            shape((planes, 2 * c1, cols), f32),
            payload,
            payload,
            shape((2, c1, LANES), f32),
        ],
        in_specs=[vmem] * 3,
        out_specs=[vmem] * 5,
        scratch_shapes=band_scratch
        + [
            pltpu.VMEM((3, 9 * c1, cols), f32),
            pltpu.SMEM((1, LANES), f32),
            pltpu.SemaphoreType.DMA,
        ],
        compiler_params=params,
        name="edge_rows",
    )(kernel_edge, arrived, ref_features)
    far = swapped(far, "view", 1)
    near = swapped(near, "view", 0)

    partial, own_top, choices = pl.pallas_call(
        functools.partial(mid_kernel, at_slots, at_live, sources, blocks, mid_blocks),
        out_shape=[
            shape((half_p, half_r * c2, half_x), f32),
            shape((planes, c1, cols), f32),
            shape((cols, 2 * col_step), bf16),
        ],
        in_specs=[anywhere] + [vmem] * 7,
        out_specs=[vmem] * 3,
        scratch_shapes=band_scratch
        + [
            pltpu.VMEM((planes * inner, cols), bf16),
            pltpu.VMEM((3, 3 * (inner + c1), cols), f32),
            pltpu.SMEM(scalars.shape, i32),
            pltpu.SemaphoreType.DMA,
        ],
        compiler_params=params,
        name="middle_rows",
    )(scalars, arrived, ref_features, edge_var, kernel_mid, bias_rows, two_mid, bias_two)

    out = pl.pallas_call(
        end_kernel,
        out_shape=shape((half_p, half_r * c2, half_x), f32),
        in_specs=[vmem] * 9,
        out_specs=vmem,
        compiler_params=params,
        name="end_rows",
    )(far, near, flags, own, own_top, partial, bias_rows, two_edge, choices)
    return out.reshape(half_p, half_r, c2, half_x)


def solution(mesh):
    return jax.shard_map(
        on_device,
        mesh=mesh,
        in_specs=(
            P(("groups", "view"), None, None),
            P(("groups", "view"), None, None, None),
            P(("groups", "view"), None, None),
            P(("groups", "view")),
            P("groups", None),
            P(),
            P(),
            P(),
            P(),
        ),
        out_specs=P("groups", "view", None, None),
        check_vma=False,
    )
```

profile of v0, /device:TPU:9, one launch (start us, length us, event | category | flops | bytes accessed | tf_op | source)
XLA Modules:
  0.0 62.8 jit_solution(16638125696243059723)
XLA Ops:
  0.0 0.7 %copy-done.4 = s32[1,4,4]{2,1,0:T(4,128)S(1)} copy-done((s32[1,4,4]{2,1,0:T(4,128)S(1)}, s32[1,4,4]{2,1,0:T(4,128)}, u32[]{:S(2)}) %copy-start.4) | copy-done | bytes 88
  0.8 11.1 %all_to_all.5 = s32[16,1,4]{2,1,0:T(1,128)S(1)} all-to-all(s32[16,1,4]{2,1,0:T(1,128)S(1)} %request_table.1), channel_id=1, replica_groups=mesh['groups'=2,'view'=16] {'view'}, dimensions={0} | all-to-all | bytes 512 | tf_op jit(solution)/shard_map/all_to_all | solution.py:418
  12.1 1.4 %copy-done = bf16[32,2,32,384]{3,2,1,0:T(8,128)(2,1)S(1)} copy-done((bf16[32,2,32,384]{3,2,1,0:T(8,128)(2,1)S(1)}, bf16[32,2,32,384]{3,2,1,0:T(8,128)(2,1)}, u32[]{:S(2)}) %copy-start) | copy-done | bytes 1572888
  13.5 0.7 %requested_tiles.1 = (bf16[2,64,384]{2,1,0:T(8,128)(2,1)S(1)}, bf16[2,64,384]{2,1,0:T(8,128)(2,1)S(1)}, bf16[2,64,384]{2,1,0:T(8,128)(2,1)S(1)}, bf16[2,64,384]{...) custom-call(s32[1,48]{1,0:T(1,128)S(1)} %reshape_squeeze.3.table, ...), custom_call_target="tpu_custom_call" | custom-call | tf_op jit(solution)/shard_map/requested_tiles/pallas_call | solution.py:425
  14.6 0.9 %collective-permute-start.1 = (bf16[2,64,384]{2,1,0:T(8,128)(2,1)S(1)}, bf16[2,64,384]{2,1,0:T(8,128)(2,1)S(1)}, u32[]{:S(2)}, u32[]{:S(2)}) collective-permute-start(bf16[2,64,384]{2,1,0:T(8,128)(2,1)S(1)} %get-tuple-element.38), channel_id=1, source_target_pairs={{0,15},{1,0},{2,1},{3,2},{4,3},{5,4},{6,5},{7,6},{8,7},{9,8},{10,9... | collective-permute-start | bytes 294920 | tf_op jit(solution)/shard_map/ppermute | solution.py:435
  15.5 2.6 %collective-permute-start.2 = (bf16[2,64,384]{2,1,0:T(8,128)(2,1)S(1)}, bf16[2,64,384]{2,1,0:T(8,128)(2,1)S(1)}, u32[]{:S(2)}, u32[]{:S(2)}) collective-permute-start(bf16[2,64,384]{2,1,0:T(8,128)(2,1)S(1)} %get-tuple-element.39), channel_id=1, source_target_pairs={{0,7},{1,8},{2,9},{3,10},{4,11},{5,12},{6,13},{7,14},{8,15},{9,0},... | collective-permute-start | bytes 294920 | tf_op jit(solution)/shard_map/ppermute | solution.py:435
  18.1 0.9 %collective-permute-start.3 = (bf16[2,64,384]{2,1,0:T(8,128)(2,1)S(1)}, bf16[2,64,384]{2,1,0:T(8,128)(2,1)S(1)}, u32[]{:S(2)}, u32[]{:S(2)}) collective-permute-start(bf16[2,64,384]{2,1,0:T(8,128)(2,1)S(1)} %get-tuple-element.40), channel_id=1, source_target_pairs={{0,1},{1,2},{2,3},{3,4},{4,5},{5,6},{6,7},{7,8},{8,9},{9,10},{10,1... | collective-permute-start | bytes 294920 | tf_op jit(solution)/shard_map/ppermute | solution.py:435
  19.1 8.3 %collective-permute-start.5 = (bf16[2,64,384]{2,1,0:T(8,128)(2,1)S(1)}, bf16[2,64,384]{2,1,0:T(8,128)(2,1)S(1)}, u32[]{:S(2)}, u32[]{:S(2)}) collective-permute-start(bf16[2,64,384]{2,1,0:T(8,128)(2,1)S(1)} %get-tuple-element.42), channel_id=1, source_target_pairs={{0,14},{1,15},{2,0},{3,1},{4,2},{5,3},{6,4},{7,5},{8,6},{9,7},{10,... | collective-permute-start | bytes 294920 | tf_op jit(solution)/shard_map/ppermute | solution.py:435
  27.4 2.0 %collective-permute-start.7 = (bf16[2,64,384]{2,1,0:T(8,128)(2,1)S(1)}, bf16[2,64,384]{2,1,0:T(8,128)(2,1)S(1)}, u32[]{:S(2)}, u32[]{:S(2)}) collective-permute-start(bf16[2,64,384]{2,1,0:T(8,128)(2,1)S(1)} %get-tuple-element.44), channel_id=1, source_target_pairs={{0,2},{1,3},{2,4},{3,5},{4,6},{5,7},{6,8},{7,9},{8,10},{9,11},{10,... | collective-permute-start | bytes 294920 | tf_op jit(solution)/shard_map/ppermute | solution.py:435
  29.4 4.2 %collective-permute-start.8 = (bf16[2,64,384]{2,1,0:T(8,128)(2,1)S(1)}, bf16[2,64,384]{2,1,0:T(8,128)(2,1)S(1)}, u32[]{:S(2)}, u32[]{:S(2)}) collective-permute-start(bf16[2,64,384]{2,1,0:T(8,128)(2,1)S(1)} %get-tuple-element.45), channel_id=1, source_target_pairs={{0,10},{1,11},{2,12},{3,13},{4,14},{5,15},{6,0},{7,1},{8,2},{9,3},... | collective-permute-start | bytes 294920 | tf_op jit(solution)/shard_map/ppermute | solution.py:435
  33.6 1.1 %collective-permute-start.9 = (bf16[2,64,384]{2,1,0:T(8,128)(2,1)S(1)}, bf16[2,64,384]{2,1,0:T(8,128)(2,1)S(1)}, u32[]{:S(2)}, u32[]{:S(2)}) collective-permute-start(bf16[2,64,384]{2,1,0:T(8,128)(2,1)S(1)} %get-tuple-element.46), channel_id=1, source_target_pairs={{0,13},{1,14},{2,15},{3,0},{4,1},{5,2},{6,3},{7,4},{8,5},{9,6},{10... | collective-permute-start | bytes 294920 | tf_op jit(solution)/shard_map/ppermute | solution.py:435
  34.7 1.8 %collective-permute-start.11 = (bf16[2,64,384]{2,1,0:T(8,128)(2,1)S(1)}, bf16[2,64,384]{2,1,0:T(8,128)(2,1)S(1)}, u32[]{:S(2)}, u32[]{:S(2)}) collective-permute-start(bf16[2,64,384]{2,1,0:T(8,128)(2,1)S(1)} %get-tuple-element.48), channel_id=1, source_target_pairs={{0,3},{1,4},{2,5},{3,6},{4,7},{5,8},{6,9},{7,10},{8,11},{9,12},{10... | collective-permute-start | bytes 294920 | tf_op jit(solution)/shard_map/ppermute | solution.py:435
  36.4 1.4 %collective-permute-done.7.refs_7_ = bf16[2,64,384]{2,1,0:T(8,128)(2,1)S(1)} collective-permute-done((bf16[2,64,384]{2,1,0:T(8,128)(2,1)S(1)}, bf16[2,64,384]{2,1,0:T(8,128)(2,1)S(1)}, u32[]{:S(2)}, u32[]{:S(2)}) %collective-permute-start.7) | collective-permute-done | bytes 98336 | tf_op jit(solution)/shard_map/ppermute | solution.py:435
  37.9 1.7 %collective-permute-start.12 = (bf16[2,64,384]{2,1,0:T(8,128)(2,1)S(1)}, bf16[2,64,384]{2,1,0:T(8,128)(2,1)S(1)}, u32[]{:S(2)}, u32[]{:S(2)}) collective-permute-start(bf16[2,64,384]{2,1,0:T(8,128)(2,1)S(1)} %get-tuple-element.49), channel_id=1, source_target_pairs={{0,11},{1,12},{2,13},{3,14},{4,15},{5,0},{6,1},{7,2},{8,3},{9,4},{... | collective-permute-start | bytes 294920 | tf_op jit(solution)/shard_map/ppermute | solution.py:435
  39.9 5.0 %collective-permute-done.9.refs_9_ = bf16[2,64,384]{2,1,0:T(8,128)(2,1)S(1)} collective-permute-done((bf16[2,64,384]{2,1,0:T(8,128)(2,1)S(1)}, bf16[2,64,384]{2,1,0:T(8,128)(2,1)S(1)}, u32[]{:S(2)}, u32[]{:S(2)}) %collective-permute-start.9) | collective-permute-done | bytes 98336 | tf_op jit(solution)/shard_map/ppermute | solution.py:435
  45.6 1.7 %weights_and_scalars.1 = (f32[224,128]{1,0:T(8,128)S(1)}, f32[504,256]{1,0:T(8,128)S(1)}, bf16[192,256]{1,0:T(8,128)(2,1)S(1)}, bf16[192,128]{1,0:T(8,128)(2,1)S...) custom-call(bf16[3,3,3,8,32]{4,3,2,1,0:T(8,128)(2,1)S(1)} %bitcast.6, ...), custom_call_target="tpu_custom_call" | custom-call | tf_op jit(solution)/shard_map/weights_and_scalars/pallas_call | solution.py:444
  48.0 0.8 %collective-permute-done.12.refs_12_ = bf16[2,64,384]{2,1,0:T(8,128)(2,1)S(1)} collective-permute-done((bf16[2,64,384]{2,1,0:T(8,128)(2,1)S(1)}, bf16[2,64,384]{2,1,0:T(8,128)(2,1)S(1)}, u32[]{:S(2)}, u32[]{:S(2)}) %collective-permute-start.12) | collective-permute-done | bytes 98336 | tf_op jit(solution)/shard_map/ppermute | solution.py:435
  48.8 2.8 %collective-permute-done.13.refs_13_ = bf16[2,64,384]{2,1,0:T(8,128)(2,1)S(1)} collective-permute-done((bf16[2,64,384]{2,1,0:T(8,128)(2,1)S(1)}, bf16[2,64,384]{2,1,0:T(8,128)(2,1)S(1)}, u32[]{:S(2)}, u32[]{:S(2)}) %collective-permute-start.13) | collective-permute-done | bytes 98336 | tf_op jit(solution)/shard_map/ppermute | solution.py:435
  51.7 0.8 %copy-done.1 = bf16[8,32,384]{2,1,0:T(8,128)(2,1)S(1)} copy-done((bf16[8,32,384]{2,1,0:T(8,128)(2,1)S(1)}, bf16[8,32,384]{2,1,0:T(8,128)(2,1)}, u32[]{:S(2)}) %copy-start.1) | copy-done | bytes 196632
  52.5 2.1 %edge_rows.1 = (bf16[8,384,128]{2,1,0:T(8,128)(2,1)S(1)}, f32[8,16,384]{2,1,0:T(8,128)S(1)}, bf16[8,16,384]{2,1,0:T(8,128)(2,1)S(1)}, bf16[8,16,384]{2,1,0:T(8,128)(2,1)S(1)}, f32[2,8,128]{2,1,0:T(8,128)S(1)}) custom-call(f32[224,128]{1,0:T(8,128)S(1)} %get-tuple-element.36.packed, bf16[32,64,384]{2,1,0:T(8,128)(2,1)S(1)} %all_tiles.1.arrived, ...), custom_call_target="tpu_custom_call" | custom-call | tf_op jit(solution)/shard_map/edge_rows/pallas_call | solution.py:483
  54.6 2.9 %collective-permute-start.15 = (bf16[8,16,384]{2,1,0:T(8,128)(2,1)S(1)}, bf16[8,16,384]{2,1,0:T(8,128)(2,1)S(1)}, u32[]{:S(2)}, u32[]{:S(2)}) collective-permute-start(bf16[8,16,384]{2,1,0:T(8,128)(2,1)S(1)} %get-tuple-element.53), channel_id=1, source_target_pairs={{1,2},{3,4},{5,6},{7,8},{9,10},{11,12},{13,14},{2,1},{4,3},{6,5},{... | collective-permute-start | bytes 294920 | tf_op jit(solution)/shard_map/ppermute | solution.py:22
  57.6 2.9 %middle_rows.1 = (f32[4,64,192]{2,1,0:T(8,128)S(1)}, f32[8,8,384]{2,1,0:T(8,128)S(1)}, bf16[384,512]{1,0:T(8,128)(2,1)S(1)}) custom-call(s32[128]{0:T(128)S(1)} %get-tuple-element.57.numbers, bf16[32,64,384]{2,1,0:T(8,128)(2,1)S(1)} %all_tiles.1.arrived, bf16[8,32,384]{2,1,0:T(8,128)(2,1)S(1)} %copy-done.1, ...), custom_call_target="tpu_custom_call" | custom-call | tf_op jit(solution)/shard_map/middle_rows/pallas_call | solution.py:506
  60.6 1.0 %collective-permute-done.15.far = bf16[8,16,384]{2,1,0:T(8,128)(2,1)S(1)} collective-permute-done((bf16[8,16,384]{2,1,0:T(8,128)(2,1)S(1)}, bf16[8,16,384]{2,1,0:T(8,128)(2,1)S(1)}, u32[]{:S(2)}, u32[]{:S(2)}) %collective-permute-start.15) | collective-permute-done | bytes 98336 | tf_op jit(solution)/shard_map/ppermute | solution.py:22
  61.6 1.3 %end_rows.1 = f32[4,64,192]{2,1,0:T(8,128)} custom-call(bf16[8,16,384]{2,1,0:T(8,128)(2,1)S(1)} %collective-permute-done.15.far, bf16[8,16,384]{2,1,0:T(8,128)(2,1)S(1)} %collective-permute-done.16.near, f32[2,8,128]{2,1,0:T(8,128)S(1)} %get-tuple-element.55.flags, f32[8,16,384]{2,1,0:T(8,128)S(1)} %get-tuple-element.56.own, ...), custom_call_target="tpu_custom_call" | custom-call | tf_op jit(solution)/shard_map/end_rows/pallas_call | solution.py:526
  (39 shorter events, 2.0 us)
Async XLA Ops:
  0.7 44.8 %copy-start.8 = (s32[8,4]{0,1:T(4,128)S(1)}, s32[8,4]{0,1:T(4,128)}, u32[]{:S(2)}) copy-start(s32[8,4]{0,1:T(4,128)} %param.13) | copy-start | bytes 388
  0.7 44.9 %copy-start.5 = (s32[1,4,4]{2,1,0:T(4,128)S(1)}, s32[1,4,4]{2,1,0:T(4,128)}, u32[]{:S(2)}) copy-start(s32[1,4,4]{2,1,0:T(4,128)} %pair_lists.3) | copy-start | bytes 196
  0.7 44.9 %copy-start.6 = (f32[8]{0:T(128)S(1)}, f32[8]{0:T(128)}, u32[]{:S(2)}) copy-start(f32[8]{0:T(128)} %bias_first.1) | copy-start | bytes 100
  0.7 44.9 %copy-start.7 = (f32[16]{0:T(128)S(1)}, f32[16]{0:T(128)}, u32[]{:S(2)}) copy-start(f32[16]{0:T(128)} %bias_second.1) | copy-start | bytes 196
  12.1 1.4 %copy-start = (bf16[32,2,32,384]{3,2,1,0:T(8,128)(2,1)S(1)}, bf16[32,2,32,384]{3,2,1,0:T(8,128)(2,1)}, u32[]{:S(2)}) copy-start(bf16[32,2,32,384]{3,2,1,0:T(8,128)(2,1)} %param.10) | copy-start | bytes 4718596
  13.5 32.2 %copy-start.2 = (bf16[3,3,8,3,32]{4,2,3,1,0:T(8,128)(2,1)S(1)}, bf16[3,3,8,3,32]{4,2,3,1,0:T(8,128)(2,1)}, u32[]{:S(2)}) copy-start(bf16[3,3,8,3,32]{4,2,3,1,0:T(8,128)(2,1)} %param.14) | copy-start | bytes 41476
  13.5 32.2 %copy-start.3 = (bf16[16,3,3,3,8]{0,4,3,2,1:T(8,128)(2,1)S(1)}, bf16[16,3,3,3,8]{0,4,3,2,1:T(8,128)(2,1)}, u32[]{:S(2)}) copy-start(bf16[16,3,3,3,8]{0,4,3,2,1:T(8,128)(2,1)} %param.16) | copy-start | bytes 20740
  14.2 4.9 %collective-permute-start = (bf16[2,64,384]{2,1,0:T(8,128)(2,1)S(1)}, bf16[2,64,384]{2,1,0:T(8,128)(2,1)S(1)}, u32[]{:S(2)}, u32[]{:S(2)}) collective-permute-start(bf16[2,64,384]{2,1,0:T(8,128)(2,1)S(1)} %get-tuple-element.37), channel_id=1, source_target_pairs={{0,8},{1,9},{2,10},{3,11},{4,12},{5,13},{6,14},{7,15},{8,0},{9,1},... | collective-permute-start | bytes 294920 | tf_op jit(solution)/shard_map/ppermute | solution.py:435
  14.6 12.8 %collective-permute-start.1 = (bf16[2,64,384]{2,1,0:T(8,128)(2,1)S(1)}, bf16[2,64,384]{2,1,0:T(8,128)(2,1)S(1)}, u32[]{:S(2)}, u32[]{:S(2)}) collective-permute-start(bf16[2,64,384]{2,1,0:T(8,128)(2,1)S(1)} %get-tuple-element.38), channel_id=1, source_target_pairs={{0,15},{1,0},{2,1},{3,2},{4,3},{5,4},{6,5},{7,6},{8,7},{9,8},{10,9... | collective-permute-start | bytes 294920 | tf_op jit(solution)/shard_map/ppermute | solution.py:435
  15.5 11.9 %collective-permute-start.2 = (bf16[2,64,384]{2,1,0:T(8,128)(2,1)S(1)}, bf16[2,64,384]{2,1,0:T(8,128)(2,1)S(1)}, u32[]{:S(2)}, u32[]{:S(2)}) collective-permute-start(bf16[2,64,384]{2,1,0:T(8,128)(2,1)S(1)} %get-tuple-element.39), channel_id=1, source_target_pairs={{0,7},{1,8},{2,9},{3,10},{4,11},{5,12},{6,13},{7,14},{8,15},{9,0},... | collective-permute-start | bytes 294920 | tf_op jit(solution)/shard_map/ppermute | solution.py:435
  18.1 11.3 %collective-permute-start.3 = (bf16[2,64,384]{2,1,0:T(8,128)(2,1)S(1)}, bf16[2,64,384]{2,1,0:T(8,128)(2,1)S(1)}, u32[]{:S(2)}, u32[]{:S(2)}) collective-permute-start(bf16[2,64,384]{2,1,0:T(8,128)(2,1)S(1)} %get-tuple-element.40), channel_id=1, source_target_pairs={{0,1},{1,2},{2,3},{3,4},{4,5},{5,6},{6,7},{7,8},{8,9},{9,10},{10,1... | collective-permute-start | bytes 294920 | tf_op jit(solution)/shard_map/ppermute | solution.py:435
  19.0 14.5 %collective-permute-start.4 = (bf16[2,64,384]{2,1,0:T(8,128)(2,1)S(1)}, bf16[2,64,384]{2,1,0:T(8,128)(2,1)S(1)}, u32[]{:S(2)}, u32[]{:S(2)}) collective-permute-start(bf16[2,64,384]{2,1,0:T(8,128)(2,1)S(1)} %get-tuple-element.41), channel_id=1, source_target_pairs={{0,9},{1,10},{2,11},{3,12},{4,13},{5,14},{6,15},{7,0},{8,1},{9,2},... | collective-permute-start | bytes 294920 | tf_op jit(solution)/shard_map/ppermute | solution.py:435
  19.1 15.6 %collective-permute-start.5 = (bf16[2,64,384]{2,1,0:T(8,128)(2,1)S(1)}, bf16[2,64,384]{2,1,0:T(8,128)(2,1)S(1)}, u32[]{:S(2)}, u32[]{:S(2)}) collective-permute-start(bf16[2,64,384]{2,1,0:T(8,128)(2,1)S(1)} %get-tuple-element.42), channel_id=1, source_target_pairs={{0,14},{1,15},{2,0},{3,1},{4,2},{5,3},{6,4},{7,5},{8,6},{9,7},{10,... | collective-permute-start | bytes 294920 | tf_op jit(solution)/shard_map/ppermute | solution.py:435
  27.4 7.3 %collective-permute-start.6 = (bf16[2,64,384]{2,1,0:T(8,128)(2,1)S(1)}, bf16[2,64,384]{2,1,0:T(8,128)(2,1)S(1)}, u32[]{:S(2)}, u32[]{:S(2)}) collective-permute-start(bf16[2,64,384]{2,1,0:T(8,128)(2,1)S(1)} %get-tuple-element.43), channel_id=1, source_target_pairs={{0,6},{1,7},{2,8},{3,9},{4,10},{5,11},{6,12},{7,13},{8,14},{9,15},... | collective-permute-start | bytes 294920 | tf_op jit(solution)/shard_map/ppermute | solution.py:435
  27.4 10.5 %collective-permute-start.7 = (bf16[2,64,384]{2,1,0:T(8,128)(2,1)S(1)}, bf16[2,64,384]{2,1,0:T(8,128)(2,1)S(1)}, u32[]{:S(2)}, u32[]{:S(2)}) collective-permute-start(bf16[2,64,384]{2,1,0:T(8,128)(2,1)S(1)} %get-tuple-element.44), channel_id=1, source_target_pairs={{0,2},{1,3},{2,4},{3,5},{4,6},{5,7},{6,8},{7,9},{8,10},{9,11},{10,... | collective-permute-start | bytes 294920 | tf_op jit(solution)/shard_map/ppermute | solution.py:435
  29.4 10.2 %collective-permute-start.8 = (bf16[2,64,384]{2,1,0:T(8,128)(2,1)S(1)}, bf16[2,64,384]{2,1,0:T(8,128)(2,1)S(1)}, u32[]{:S(2)}, u32[]{:S(2)}) collective-permute-start(bf16[2,64,384]{2,1,0:T(8,128)(2,1)S(1)} %get-tuple-element.45), channel_id=1, source_target_pairs={{0,10},{1,11},{2,12},{3,13},{4,14},{5,15},{6,0},{7,1},{8,2},{9,3},... | collective-permute-start | bytes 294920 | tf_op jit(solution)/shard_map/ppermute | solution.py:435
  33.6 11.3 %collective-permute-start.9 = (bf16[2,64,384]{2,1,0:T(8,128)(2,1)S(1)}, bf16[2,64,384]{2,1,0:T(8,128)(2,1)S(1)}, u32[]{:S(2)}, u32[]{:S(2)}) collective-permute-start(bf16[2,64,384]{2,1,0:T(8,128)(2,1)S(1)} %get-tuple-element.46), channel_id=1, source_target_pairs={{0,13},{1,14},{2,15},{3,0},{4,1},{5,2},{6,3},{7,4},{8,5},{9,6},{10... | collective-permute-start | bytes 294920 | tf_op jit(solution)/shard_map/ppermute | solution.py:435
  34.7 12.7 %collective-permute-start.10 = (bf16[2,64,384]{2,1,0:T(8,128)(2,1)S(1)}, bf16[2,64,384]{2,1,0:T(8,128)(2,1)S(1)}, u32[]{:S(2)}, u32[]{:S(2)}) collective-permute-start(bf16[2,64,384]{2,1,0:T(8,128)(2,1)S(1)} %get-tuple-element.47), channel_id=1, source_target_pairs={{0,5},{1,6},{2,7},{3,8},{4,9},{5,10},{6,11},{7,12},{8,13},{9,14},{... | collective-permute-start | bytes 294920 | tf_op jit(solution)/shard_map/ppermute | solution.py:435
  34.7 13.4 %collective-permute-start.11 = (bf16[2,64,384]{2,1,0:T(8,128)(2,1)S(1)}, bf16[2,64,384]{2,1,0:T(8,128)(2,1)S(1)}, u32[]{:S(2)}, u32[]{:S(2)}) collective-permute-start(bf16[2,64,384]{2,1,0:T(8,128)(2,1)S(1)} %get-tuple-element.48), channel_id=1, source_target_pairs={{0,3},{1,4},{2,5},{3,6},{4,7},{5,8},{6,9},{7,10},{8,11},{9,12},{10... | collective-permute-start | bytes 294920 | tf_op jit(solution)/shard_map/ppermute | solution.py:435
  37.9 10.9 %collective-permute-start.12 = (bf16[2,64,384]{2,1,0:T(8,128)(2,1)S(1)}, bf16[2,64,384]{2,1,0:T(8,128)(2,1)S(1)}, u32[]{:S(2)}, u32[]{:S(2)}) collective-permute-start(bf16[2,64,384]{2,1,0:T(8,128)(2,1)S(1)} %get-tuple-element.49), channel_id=1, source_target_pairs={{0,11},{1,12},{2,13},{3,14},{4,15},{5,0},{6,1},{7,2},{8,3},{9,4},{... | collective-permute-start | bytes 294920 | tf_op jit(solution)/shard_map/ppermute | solution.py:435
  39.6 12.0 %collective-permute-start.13 = (bf16[2,64,384]{2,1,0:T(8,128)(2,1)S(1)}, bf16[2,64,384]{2,1,0:T(8,128)(2,1)S(1)}, u32[]{:S(2)}, u32[]{:S(2)}) collective-permute-start(bf16[2,64,384]{2,1,0:T(8,128)(2,1)S(1)} %get-tuple-element.50), channel_id=1, source_target_pairs={{0,12},{1,13},{2,14},{3,15},{4,0},{5,1},{6,2},{7,3},{8,4},{9,5},{1... | collective-permute-start | bytes 294920 | tf_op jit(solution)/shard_map/ppermute | solution.py:435
  44.9 6.7 %collective-permute-start.14 = (bf16[2,64,384]{2,1,0:T(8,128)(2,1)S(1)}, bf16[2,64,384]{2,1,0:T(8,128)(2,1)S(1)}, u32[]{:S(2)}, u32[]{:S(2)}) collective-permute-start(bf16[2,64,384]{2,1,0:T(8,128)(2,1)S(1)} %get-tuple-element.51), channel_id=1, source_target_pairs={{0,4},{1,5},{2,6},{3,7},{4,8},{5,9},{6,10},{7,11},{8,12},{9,13},{1... | collective-permute-start | bytes 294920 | tf_op jit(solution)/shard_map/ppermute | solution.py:435
  54.6 7.0 %collective-permute-start.15 = (bf16[8,16,384]{2,1,0:T(8,128)(2,1)S(1)}, bf16[8,16,384]{2,1,0:T(8,128)(2,1)S(1)}, u32[]{:S(2)}, u32[]{:S(2)}) collective-permute-start(bf16[8,16,384]{2,1,0:T(8,128)(2,1)S(1)} %get-tuple-element.53), channel_id=1, source_target_pairs={{1,2},{3,4},{5,6},{7,8},{9,10},{11,12},{13,14},{2,1},{4,3},{6,5},{... | collective-permute-start | bytes 294920 | tf_op jit(solution)/shard_map/ppermute | solution.py:22
  57.5 4.1 %collective-permute-start.16 = (bf16[8,16,384]{2,1,0:T(8,128)(2,1)S(1)}, bf16[8,16,384]{2,1,0:T(8,128)(2,1)S(1)}, u32[]{:S(2)}, u32[]{:S(2)}) collective-permute-start(bf16[8,16,384]{2,1,0:T(8,128)(2,1)S(1)} %get-tuple-element.54), channel_id=1, source_target_pairs={{0,1},{2,3},{4,5},{6,7},{8,9},{10,11},{12,13},{14,15},{1,0},{3,2},... | collective-permute-start | bytes 294920 | tf_op jit(solution)/shard_map/ppermute | solution.py:22
  (2 other events, 1.6 us)
where the time goes:
time: 63.6 us; the launch traced here: 62.8 us
  starting transfers between devices  27.2 us (43%)
  waiting for transfers between devices  11.7 us (18%)
  blocking collectives  11.1 us (17%)
  Pallas kernels  8.97 us (14%)
  local copies, waits for them, and re-layouts  3.08 us (5%)
  between operations  0.79 us (1%)
    ppermute x15, starting transfers between devices, on_device(): bundles[k] = lax.ppermute(bundle, 'view', pairs) if k else bundle  24.2 us
    all_to_all x1, blocking collectives, on_device(): lax.all_to_all(table, 'view', split_axis=0, concat_axis=0, tiled=True)  11.1 us
    ppermute x15, waiting for transfers between devices, on_device(): bundles[k] = lax.ppermute(bundle, 'view', pairs) if k else bundle  10.7 us
    ppermute x2, starting transfers between devices, swapped(): return lax.ppermute(x, axis, pairs + [(j, i) for i, j in pairs])  3 us
    unnamed x19, local copies, waits for them, and re-layouts  2.98 us
    pallas_call x1, Pallas kernels, on_device(): pl.pallas_call(functools.partial(mid_kernel, at_slots, at_live, sources,...  2.95 us
    pallas_call x1, Pallas kernels, on_device(): pl.pallas_call(functools.partial(edge_kernel, at_slots, at_live, sources,...  2.06 us
    pallas_call x1, Pallas kernels, on_device(): pl.pallas_call(functools.partial(prepare_kernel, n_view, tiles_dev, edge_...  1.72 us
  transfers between devices with their start and end apart: 17, of which 6 were waited for; matrix products, arithmetic and copies ran while one was open for 0% of the time, Pallas kernels for 7%

commit v1 on v0

--- a/solution.py
+++ b/solution.py
@@ -55,7 +55,7 @@
         table[d] = total[d : d + 1, : table.shape[2]]
 
 
-def gather_kernel(distances, n_view, table, tiles, *bundles):
+def gather_kernel(distances, n_view, table, tiles, _, *bundles):
     me = table[0, CAP]
     for k, bundle in zip(distances, bundles):
         at = lax.rem(me + k, n_view) * (CAP + 1)
@@ -416,24 +416,6 @@
         name="request_table",
     )(pair_lists)
     table = lax.all_to_all(table, "view", split_axis=0, concat_axis=0, tiled=True)
-    tiles = source_tiles.reshape(tiles_dev, slab, cols)
-    table = table[:, 0, : CAP + 1].reshape(1, n_view * (CAP + 1))
-    far_first = sorted(range(1, n_view), key=lambda k: -min(k, n_view - k))
-    order = [k for pair in zip(far_first, far_first[::-1]) for k in pair][: len(far_first)]
-    distances = order + [0]
-    bundles = [None] * n_view
-    gathered = pl.pallas_call(
-        functools.partial(gather_kernel, distances, n_view),
-        out_shape=[shape((CAP, slab, cols), bf16)] * n_view,
-        in_specs=[smem, vmem],
-        out_specs=[vmem] * n_view,
-        compiler_params=params,
-        name="requested_tiles",
-    )(table, tiles)
-    for k, bundle in zip(distances, gathered):
-        pairs = [(i, (i + k) % n_view) for i in range(n_view)]
-        bundles[k] = lax.ppermute(bundle, "view", pairs) if k else bundle
-
     at_slots = planes * sources
     at_live = at_slots + sources * blocks
     edge_blocks, mid_blocks = (0, blocks - 1), tuple(range(1, blocks - 1))
@@ -468,6 +450,24 @@
         me,
     )
     kernel_edge, kernel_mid, two_mid, two_edge, bias_rows, bias_two, scalars = prepared
+
+    tiles = source_tiles.reshape(tiles_dev, slab, cols)
+    table = table[:, 0, : CAP + 1].reshape(1, n_view * (CAP + 1))
+    far_first = sorted(range(1, n_view), key=lambda k: -min(k, n_view - k))
+    order = [k for pair in zip(far_first, far_first[::-1]) for k in pair][: len(far_first)]
+    distances = order + [0]
+    bundles = [None] * n_view
+    gathered = pl.pallas_call(
+        functools.partial(gather_kernel, distances, n_view),
+        out_shape=[shape((CAP, slab, cols), bf16)] * n_view,
+        in_specs=[smem, vmem, anywhere],
+        out_specs=[vmem] * n_view,
+        compiler_params=params,
+        name="requested_tiles",
+    )(table, tiles, bias_two)
+    for k, bundle in zip(distances, gathered):
+        pairs = [(i, (i + k) % n_view) for i in range(n_view)]
+        bundles[k] = lax.ppermute(bundle, "view", pairs) if k else bundle
     arrived = pl.pallas_call(
         functools.partial(collect_kernel, distances),
         out_shape=shape((n_view * CAP, slab, cols), bf16),

time: 63.6 us -> 67.4 us (1.060)
  blocking collectives: 11.1 us -> 0 us
  waiting for transfers between devices: 11.7 us -> 17.3 us
  starting transfers between devices: 27.2 us -> 31.7 us
  local copies, waits for them, and re-layouts: 3.08 us -> 7.36 us
    all_to_all x1 -> x0, blocking collectives: 11.1 us -> none  [on_device(): lax.all_to_all(table, 'view', split_axis=0, concat_axis=0, tiled=True)]
    all_to_all x0 -> x1, starting transfers between devices: none -> 6.61 us  [on_device(): lax.all_to_all(table, 'view', split_axis=0, concat_axis=0, tiled=True)]
    ppermute x15, waiting for transfers between devices: 10.7 us -> 17 us  [on_device(): bundles[k] = lax.ppermute(bundle, 'view', pairs) if k else bundle]
    unnamed x19 -> x17, local copies, waits for them, and re-layouts: 2.98 us -> 7.25 us
    ppermute x15, starting transfers between devices: 24.2 us -> 21.3 us  [on_device(): bundles[k] = lax.ppermute(bundle, 'view', pairs) if k else bundle]
    ppermute x2, starting transfers between devices: 3 us -> 3.79 us  [swapped(): return lax.ppermute(x, axis, pairs + [(j, i) for i, j in pairs])]
    ppermute x2, waiting for transfers between devices: 1.02 us -> 0.31 us  [swapped(): return lax.ppermute(x, axis, pairs + [(j, i) for i, j in pairs])]
  transfers between devices with their start and end apart: 17 -> 18, of which waited for: 6 -> 6; matrix products, arithmetic and copies ran while one was open for 0% -> 1% of each run, Pallas kernels for 7% -> 7%
where the time goes in v1:
time: 67.4 us; the launch traced here: 66.7 us
  starting transfers between devices  31.7 us (47%)
  waiting for transfers between devices  17.3 us (26%)
  Pallas kernels  9.56 us (14%)
  local copies, waits for them, and re-layouts  7.36 us (11%)
  between operations  0.76 us (1%)
    ppermute x15, starting transfers between devices, on_device(): bundles[k] = lax.ppermute(bundle, 'view', pairs) if k else bundle  21.3 us
    ppermute x15, waiting for transfers between devices, on_device(): bundles[k] = lax.ppermute(bundle, 'view', pairs) if k else bundle  17 us
    unnamed x17, local copies, waits for them, and re-layouts  7.25 us
    all_to_all x1, starting transfers between devices, on_device(): lax.all_to_all(table, 'view', split_axis=0, concat_axis=0, tiled=True)  6.61 us
    ppermute x2, starting transfers between devices, swapped(): return lax.ppermute(x, axis, pairs + [(j, i) for i, j in pairs])  3.79 us
    pallas_call x1, Pallas kernels, on_device(): pl.pallas_call(functools.partial(mid_kernel, at_slots, at_live, sources,...  2.94 us
    pallas_call x1, Pallas kernels, on_device(): pl.pallas_call(functools.partial(edge_kernel, at_slots, at_live, sources,...  2.07 us
    pallas_call x1, Pallas kernels, on_device(): pl.pallas_call(functools.partial(prepare_kernel, n_view, tiles_dev, edge_...  1.71 us
  transfers between devices with their start and end apart: 18, of which 6 were waited for; matrix products, arithmetic and copies ran while one was open for 1% of the time, Pallas kernels for 7%

profile of v1, /device:TPU:9, one launch (start us, length us, event | category | flops | bytes accessed | tf_op | source)
XLA Modules:
  0.0 66.7 jit_solution(12477372052161355655)
XLA Ops:
  1.4 6.6 %all-to-all-start = ((s32[16,1,4]{2,1,0:T(1,128)}), s32[16,1,4]{2,1,0:T(1,128)S(1)}, u32[]{:S(2)}, u32[]{:S(2)}) async-start(s32[16,1,4]{2,1,0:T(1,128)} %request_table.1), calls=%async_computation | async-start | bytes 16384 | tf_op jit(solution)/shard_map/all_to_all | solution.py:418
  8.7 0.8 %copy.11.disparities = s32[8,4]{1,0:T(8,128)S(1)} copy(s32[8,4]{0,1:T(4,128)} %param.13) | data formatting | bytes 256 | tf_op args[4]
  9.4 0.8 %copy-done.2 = bf16[3,3,8,3,32]{4,2,3,1,0:T(8,128)(2,1)S(1)} copy-done((bf16[3,3,8,3,32]{4,2,3,1,0:T(8,128)(2,1)S(1)}, bf16[3,3,8,3,32]{4,2,3,1,0:T(8,128)(2,1)}, u32[]{:S(2)}) %copy-start.2) | copy-done | bytes 13848
  10.3 0.8 %copy-done.3 = bf16[16,3,3,3,8]{0,4,3,2,1:T(8,128)(2,1)S(1)} copy-done((bf16[16,3,3,3,8]{0,4,3,2,1:T(8,128)(2,1)S(1)}, bf16[16,3,3,3,8]{0,4,3,2,1:T(8,128)(2,1)}, u32[]{:S(2)}) %copy-start.3) | copy-done | bytes 6936
  13.1 1.7 %weights_and_scalars.1 = (f32[224,128]{1,0:T(8,128)S(1)}, f32[504,256]{1,0:T(8,128)S(1)}, bf16[192,256]{1,0:T(8,128)(2,1)S(1)}, bf16[192,128]{1,0:T(8,128)(2,1)S...) custom-call(bf16[3,3,3,8,32]{4,3,2,1,0:T(8,128)(2,1)S(1)} %bitcast.6, ...), custom_call_target="tpu_custom_call" | custom-call | tf_op jit(solution)/shard_map/weights_and_scalars/pallas_call | solution.py:426
  14.9 1.4 %copy-done = bf16[32,2,32,384]{3,2,1,0:T(8,128)(2,1)S(1)} copy-done((bf16[32,2,32,384]{3,2,1,0:T(8,128)(2,1)S(1)}, bf16[32,2,32,384]{3,2,1,0:T(8,128)(2,1)}, u32[]{:S(2)}) %copy-start) | copy-done | bytes 1572888
  17.0 2.2 %collective-permute-start = (bf16[2,64,384]{2,1,0:T(8,128)(2,1)S(1)}, bf16[2,64,384]{2,1,0:T(8,128)(2,1)S(1)}, u32[]{:S(2)}, u32[]{:S(2)}) collective-permute-start(bf16[2,64,384]{2,1,0:T(8,128)(2,1)S(1)} %get-tuple-element.38), channel_id=1, source_target_pairs={{0,8},{1,9},{2,10},{3,11},{4,12},{5,13},{6,14},{7,15},{8,0},{9,1},... | collective-permute-start | bytes 294920 | tf_op jit(solution)/shard_map/ppermute | solution.py:470
  19.8 1.1 %collective-permute-start.2 = (bf16[2,64,384]{2,1,0:T(8,128)(2,1)S(1)}, bf16[2,64,384]{2,1,0:T(8,128)(2,1)S(1)}, u32[]{:S(2)}, u32[]{:S(2)}) collective-permute-start(bf16[2,64,384]{2,1,0:T(8,128)(2,1)S(1)} %get-tuple-element.40), channel_id=1, source_target_pairs={{0,7},{1,8},{2,9},{3,10},{4,11},{5,12},{6,13},{7,14},{8,15},{9,0},... | collective-permute-start | bytes 294920 | tf_op jit(solution)/shard_map/ppermute | solution.py:470
  21.6 1.8 %collective-permute-start.4 = (bf16[2,64,384]{2,1,0:T(8,128)(2,1)S(1)}, bf16[2,64,384]{2,1,0:T(8,128)(2,1)S(1)}, u32[]{:S(2)}, u32[]{:S(2)}) collective-permute-start(bf16[2,64,384]{2,1,0:T(8,128)(2,1)S(1)} %get-tuple-element.42), channel_id=1, source_target_pairs={{0,9},{1,10},{2,11},{3,12},{4,13},{5,14},{6,15},{7,0},{8,1},{9,2},... | collective-permute-start | bytes 294920 | tf_op jit(solution)/shard_map/ppermute | solution.py:470
  23.4 4.5 %collective-permute-done.refs_0_ = bf16[2,64,384]{2,1,0:T(8,128)(2,1)S(1)} collective-permute-done((bf16[2,64,384]{2,1,0:T(8,128)(2,1)S(1)}, bf16[2,64,384]{2,1,0:T(8,128)(2,1)S(1)}, u32[]{:S(2)}, u32[]{:S(2)}) %collective-permute-start) | collective-permute-done | bytes 98336 | tf_op jit(solution)/shard_map/ppermute | solution.py:470
  28.0 2.2 %collective-permute-done.2.refs_2_ = bf16[2,64,384]{2,1,0:T(8,128)(2,1)S(1)} collective-permute-done((bf16[2,64,384]{2,1,0:T(8,128)(2,1)S(1)}, bf16[2,64,384]{2,1,0:T(8,128)(2,1)S(1)}, u32[]{:S(2)}, u32[]{:S(2)}) %collective-permute-start.2) | collective-permute-done | bytes 98336 | tf_op jit(solution)/shard_map/ppermute | solution.py:470
  30.2 2.2 %collective-permute-start.7 = (bf16[2,64,384]{2,1,0:T(8,128)(2,1)S(1)}, bf16[2,64,384]{2,1,0:T(8,128)(2,1)S(1)}, u32[]{:S(2)}, u32[]{:S(2)}) collective-permute-start(bf16[2,64,384]{2,1,0:T(8,128)(2,1)S(1)} %get-tuple-element.45), channel_id=1, source_target_pairs={{0,2},{1,3},{2,4},{3,5},{4,6},{5,7},{6,8},{7,9},{8,10},{9,11},{10,... | collective-permute-start | bytes 294920 | tf_op jit(solution)/shard_map/ppermute | solution.py:470
  32.4 3.9 %collective-permute-start.8 = (bf16[2,64,384]{2,1,0:T(8,128)(2,1)S(1)}, bf16[2,64,384]{2,1,0:T(8,128)(2,1)S(1)}, u32[]{:S(2)}, u32[]{:S(2)}) collective-permute-start(bf16[2,64,384]{2,1,0:T(8,128)(2,1)S(1)} %get-tuple-element.46), channel_id=1, source_target_pairs={{0,10},{1,11},{2,12},{3,13},{4,14},{5,15},{6,0},{7,1},{8,2},{9,3},... | collective-permute-start | bytes 294920 | tf_op jit(solution)/shard_map/ppermute | solution.py:470
  36.3 1.9 %collective-permute-start.9 = (bf16[2,64,384]{2,1,0:T(8,128)(2,1)S(1)}, bf16[2,64,384]{2,1,0:T(8,128)(2,1)S(1)}, u32[]{:S(2)}, u32[]{:S(2)}) collective-permute-start(bf16[2,64,384]{2,1,0:T(8,128)(2,1)S(1)} %get-tuple-element.47), channel_id=1, source_target_pairs={{0,13},{1,14},{2,15},{3,0},{4,1},{5,2},{6,3},{7,4},{8,5},{9,6},{10... | collective-permute-start | bytes 294920 | tf_op jit(solution)/shard_map/ppermute | solution.py:470
  38.4 5.2 %collective-permute-start.12 = (bf16[2,64,384]{2,1,0:T(8,128)(2,1)S(1)}, bf16[2,64,384]{2,1,0:T(8,128)(2,1)S(1)}, u32[]{:S(2)}, u32[]{:S(2)}) collective-permute-start(bf16[2,64,384]{2,1,0:T(8,128)(2,1)S(1)} %get-tuple-element.50), channel_id=1, source_target_pairs={{0,11},{1,12},{2,13},{3,14},{4,15},{5,0},{6,1},{7,2},{8,3},{9,4},{... | collective-permute-start | bytes 294920 | tf_op jit(solution)/shard_map/ppermute | solution.py:470
  43.6 3.1 %collective-permute-done.8.refs_8_ = bf16[2,64,384]{2,1,0:T(8,128)(2,1)S(1)} collective-permute-done((bf16[2,64,384]{2,1,0:T(8,128)(2,1)S(1)}, bf16[2,64,384]{2,1,0:T(8,128)(2,1)S(1)}, u32[]{:S(2)}, u32[]{:S(2)}) %collective-permute-start.8) | collective-permute-done | bytes 98336 | tf_op jit(solution)/shard_map/ppermute | solution.py:470
  47.4 0.9 %collective-permute-start.14 = (bf16[2,64,384]{2,1,0:T(8,128)(2,1)S(1)}, bf16[2,64,384]{2,1,0:T(8,128)(2,1)S(1)}, u32[]{:S(2)}, u32[]{:S(2)}) collective-permute-start(bf16[2,64,384]{2,1,0:T(8,128)(2,1)S(1)} %get-tuple-element.52), channel_id=1, source_target_pairs={{0,4},{1,5},{2,6},{3,7},{4,8},{5,9},{6,10},{7,11},{8,12},{9,13},{1... | collective-permute-start | bytes 294920 | tf_op jit(solution)/shard_map/ppermute | solution.py:470
  48.3 5.2 %collective-permute-done.12.refs_12_ = bf16[2,64,384]{2,1,0:T(8,128)(2,1)S(1)} collective-permute-done((bf16[2,64,384]{2,1,0:T(8,128)(2,1)S(1)}, bf16[2,64,384]{2,1,0:T(8,128)(2,1)S(1)}, u32[]{:S(2)}, u32[]{:S(2)}) %collective-permute-start.12) | collective-permute-done | bytes 98336 | tf_op jit(solution)/shard_map/ppermute | solution.py:470
  53.4 1.9 %collective-permute-done.13.refs_13_ = bf16[2,64,384]{2,1,0:T(8,128)(2,1)S(1)} collective-permute-done((bf16[2,64,384]{2,1,0:T(8,128)(2,1)S(1)}, bf16[2,64,384]{2,1,0:T(8,128)(2,1)S(1)}, u32[]{:S(2)}, u32[]{:S(2)}) %collective-permute-start.13) | collective-permute-done | bytes 98336 | tf_op jit(solution)/shard_map/ppermute | solution.py:470
  55.5 0.8 %copy-done.1 = bf16[8,32,384]{2,1,0:T(8,128)(2,1)S(1)} copy-done((bf16[8,32,384]{2,1,0:T(8,128)(2,1)S(1)}, bf16[8,32,384]{2,1,0:T(8,128)(2,1)}, u32[]{:S(2)}) %copy-start.1) | copy-done | bytes 196632
  56.2 2.1 %edge_rows.1 = (bf16[8,384,128]{2,1,0:T(8,128)(2,1)S(1)}, f32[8,16,384]{2,1,0:T(8,128)S(1)}, bf16[8,16,384]{2,1,0:T(8,128)(2,1)S(1)}, bf16[8,16,384]{2,1,0:T(8,128)(2,1)S(1)}, f32[2,8,128]{2,1,0:T(8,128)S(1)}) custom-call(f32[224,128]{1,0:T(8,128)S(1)} %get-tuple-element.36.packed, bf16[32,64,384]{2,1,0:T(8,128)(2,1)S(1)} %all_tiles.1.arrived, ...), custom_call_target="tpu_custom_call" | custom-call | tf_op jit(solution)/shard_map/edge_rows/pallas_call | solution.py:483
  58.3 3.7 %collective-permute-start.15 = (bf16[8,16,384]{2,1,0:T(8,128)(2,1)S(1)}, bf16[8,16,384]{2,1,0:T(8,128)(2,1)S(1)}, u32[]{:S(2)}, u32[]{:S(2)}) collective-permute-start(bf16[8,16,384]{2,1,0:T(8,128)(2,1)S(1)} %get-tuple-element.54), channel_id=1, source_target_pairs={{1,2},{3,4},{5,6},{7,8},{9,10},{11,12},{13,14},{2,1},{4,3},{6,5},{... | collective-permute-start | bytes 294920 | tf_op jit(solution)/shard_map/ppermute | solution.py:22
  62.1 2.9 %middle_rows.1 = (f32[4,64,192]{2,1,0:T(8,128)S(1)}, f32[8,8,384]{2,1,0:T(8,128)S(1)}, bf16[384,512]{1,0:T(8,128)(2,1)S(1)}) custom-call(s32[128]{0:T(128)S(1)} %get-tuple-element.58.numbers, bf16[32,64,384]{2,1,0:T(8,128)(2,1)S(1)} %all_tiles.1.arrived, bf16[8,32,384]{2,1,0:T(8,128)(2,1)S(1)} %copy-done.1, ...), custom_call_target="tpu_custom_call" | custom-call | tf_op jit(solution)/shard_map/middle_rows/pallas_call | solution.py:506
  65.4 1.3 %end_rows.1 = f32[4,64,192]{2,1,0:T(8,128)} custom-call(bf16[8,16,384]{2,1,0:T(8,128)(2,1)S(1)} %collective-permute-done.15.far, bf16[8,16,384]{2,1,0:T(8,128)(2,1)S(1)} %collective-permute-done.16.near, f32[2,8,128]{2,1,0:T(8,128)S(1)} %get-tuple-element.56.flags, f32[8,16,384]{2,1,0:T(8,128)S(1)} %get-tuple-element.57.own, ...), custom_call_target="tpu_custom_call" | custom-call | tf_op jit(solution)/shard_map/end_rows/pallas_call | solution.py:526
  (38 shorter events, 6.9 us)
Async XLA Ops:
  0.0 0.7 %copy-start.4 = (s32[1,4,4]{2,1,0:T(4,128)S(1)}, s32[1,4,4]{2,1,0:T(4,128)}, u32[]{:S(2)}) copy-start(s32[1,4,4]{2,1,0:T(4,128)} %pair_lists.3) | copy-start | bytes 196
  1.4 13.4 %all-to-all-start = ((s32[16,1,4]{2,1,0:T(1,128)}), s32[16,1,4]{2,1,0:T(1,128)S(1)}, u32[]{:S(2)}, u32[]{:S(2)}) async-start(s32[16,1,4]{2,1,0:T(1,128)} %request_table.1), calls=%async_computation | async-start | bytes 16384 | tf_op jit(solution)/shard_map/all_to_all | solution.py:418
  9.4 0.8 %copy-start.2 = (bf16[3,3,8,3,32]{4,2,3,1,0:T(8,128)(2,1)S(1)}, bf16[3,3,8,3,32]{4,2,3,1,0:T(8,128)(2,1)}, u32[]{:S(2)}) copy-start(bf16[3,3,8,3,32]{4,2,3,1,0:T(8,128)(2,1)} %param.14) | copy-start | bytes 41476
  10.3 0.8 %copy-start.3 = (bf16[16,3,3,3,8]{0,4,3,2,1:T(8,128)(2,1)S(1)}, bf16[16,3,3,3,8]{0,4,3,2,1:T(8,128)(2,1)}, u32[]{:S(2)}) copy-start(bf16[16,3,3,3,8]{0,4,3,2,1:T(8,128)(2,1)} %param.16) | copy-start | bytes 20740
  11.1 0.7 %copy-start.5 = (s32[1,4,4]{2,1,0:T(4,128)S(1)}, s32[1,4,4]{2,1,0:T(4,128)}, u32[]{:S(2)}) copy-start(s32[1,4,4]{2,1,0:T(4,128)} %pair_lists.3) | copy-start | bytes 196
  14.9 1.4 %copy-start = (bf16[32,2,32,384]{3,2,1,0:T(8,128)(2,1)S(1)}, bf16[32,2,32,384]{3,2,1,0:T(8,128)(2,1)}, u32[]{:S(2)}) copy-start(bf16[32,2,32,384]{3,2,1,0:T(8,128)(2,1)} %param.10) | copy-start | bytes 4718596
  17.0 10.9 %collective-permute-start = (bf16[2,64,384]{2,1,0:T(8,128)(2,1)S(1)}, bf16[2,64,384]{2,1,0:T(8,128)(2,1)S(1)}, u32[]{:S(2)}, u32[]{:S(2)}) collective-permute-start(bf16[2,64,384]{2,1,0:T(8,128)(2,1)S(1)} %get-tuple-element.38), channel_id=1, source_target_pairs={{0,8},{1,9},{2,10},{3,11},{4,12},{5,13},{6,14},{7,15},{8,0},{9,1},... | collective-permute-start | bytes 294920 | tf_op jit(solution)/shard_map/ppermute | solution.py:470
  19.2 8.8 %collective-permute-start.1 = (bf16[2,64,384]{2,1,0:T(8,128)(2,1)S(1)}, bf16[2,64,384]{2,1,0:T(8,128)(2,1)S(1)}, u32[]{:S(2)}, u32[]{:S(2)}) collective-permute-start(bf16[2,64,384]{2,1,0:T(8,128)(2,1)S(1)} %get-tuple-element.39), channel_id=1, source_target_pairs={{0,15},{1,0},{2,1},{3,2},{4,3},{5,4},{6,5},{7,6},{8,7},{9,8},{10,9... | collective-permute-start | bytes 294920 | tf_op jit(solution)/shard_map/ppermute | solution.py:470
  19.8 10.4 %collective-permute-start.2 = (bf16[2,64,384]{2,1,0:T(8,128)(2,1)S(1)}, bf16[2,64,384]{2,1,0:T(8,128)(2,1)S(1)}, u32[]{:S(2)}, u32[]{:S(2)}) collective-permute-start(bf16[2,64,384]{2,1,0:T(8,128)(2,1)S(1)} %get-tuple-element.40), channel_id=1, source_target_pairs={{0,7},{1,8},{2,9},{3,10},{4,11},{5,12},{6,13},{7,14},{8,15},{9,0},... | collective-permute-start | bytes 294920 | tf_op jit(solution)/shard_map/ppermute | solution.py:470
  20.9 11.5 %collective-permute-start.3 = (bf16[2,64,384]{2,1,0:T(8,128)(2,1)S(1)}, bf16[2,64,384]{2,1,0:T(8,128)(2,1)S(1)}, u32[]{:S(2)}, u32[]{:S(2)}) collective-permute-start(bf16[2,64,384]{2,1,0:T(8,128)(2,1)S(1)} %get-tuple-element.41), channel_id=1, source_target_pairs={{0,1},{1,2},{2,3},{3,4},{4,5},{5,6},{6,7},{7,8},{8,9},{9,10},{10,1... | collective-permute-start | bytes 294920 | tf_op jit(solution)/shard_map/ppermute | solution.py:470
  21.6 14.7 %collective-permute-start.4 = (bf16[2,64,384]{2,1,0:T(8,128)(2,1)S(1)}, bf16[2,64,384]{2,1,0:T(8,128)(2,1)S(1)}, u32[]{:S(2)}, u32[]{:S(2)}) collective-permute-start(bf16[2,64,384]{2,1,0:T(8,128)(2,1)S(1)} %get-tuple-element.42), channel_id=1, source_target_pairs={{0,9},{1,10},{2,11},{3,12},{4,13},{5,14},{6,15},{7,0},{8,1},{9,2},... | collective-permute-start | bytes 294920 | tf_op jit(solution)/shard_map/ppermute | solution.py:470
  27.9 10.2 %collective-permute-start.5 = (bf16[2,64,384]{2,1,0:T(8,128)(2,1)S(1)}, bf16[2,64,384]{2,1,0:T(8,128)(2,1)S(1)}, u32[]{:S(2)}, u32[]{:S(2)}) collective-permute-start(bf16[2,64,384]{2,1,0:T(8,128)(2,1)S(1)} %get-tuple-element.43), channel_id=1, source_target_pairs={{0,14},{1,15},{2,0},{3,1},{4,2},{5,3},{6,4},{7,5},{8,6},{9,7},{10,... | collective-permute-start | bytes 294920 | tf_op jit(solution)/shard_map/ppermute | solution.py:470
  28.0 10.2 %collective-permute-start.6 = (bf16[2,64,384]{2,1,0:T(8,128)(2,1)S(1)}, bf16[2,64,384]{2,1,0:T(8,128)(2,1)S(1)}, u32[]{:S(2)}, u32[]{:S(2)}) collective-permute-start(bf16[2,64,384]{2,1,0:T(8,128)(2,1)S(1)} %get-tuple-element.44), channel_id=1, source_target_pairs={{0,6},{1,7},{2,8},{3,9},{4,10},{5,11},{6,12},{7,13},{8,14},{9,15},... | collective-permute-start | bytes 294920 | tf_op jit(solution)/shard_map/ppermute | solution.py:470
  30.2 8.2 %collective-permute-start.7 = (bf16[2,64,384]{2,1,0:T(8,128)(2,1)S(1)}, bf16[2,64,384]{2,1,0:T(8,128)(2,1)S(1)}, u32[]{:S(2)}, u32[]{:S(2)}) collective-permute-start(bf16[2,64,384]{2,1,0:T(8,128)(2,1)S(1)} %get-tuple-element.45), channel_id=1, source_target_pairs={{0,2},{1,3},{2,4},{3,5},{4,6},{5,7},{6,8},{7,9},{8,10},{9,11},{10,... | collective-permute-start | bytes 294920 | tf_op jit(solution)/shard_map/ppermute | solution.py:470
  32.4 14.4 %collective-permute-start.8 = (bf16[2,64,384]{2,1,0:T(8,128)(2,1)S(1)}, bf16[2,64,384]{2,1,0:T(8,128)(2,1)S(1)}, u32[]{:S(2)}, u32[]{:S(2)}) collective-permute-start(bf16[2,64,384]{2,1,0:T(8,128)(2,1)S(1)} %get-tuple-element.46), channel_id=1, source_target_pairs={{0,10},{1,11},{2,12},{3,13},{4,14},{5,15},{6,0},{7,1},{8,2},{9,3},... | collective-permute-start | bytes 294920 | tf_op jit(solution)/shard_map/ppermute | solution.py:470
  36.3 11.1 %collective-permute-start.9 = (bf16[2,64,384]{2,1,0:T(8,128)(2,1)S(1)}, bf16[2,64,384]{2,1,0:T(8,128)(2,1)S(1)}, u32[]{:S(2)}, u32[]{:S(2)}) collective-permute-start(bf16[2,64,384]{2,1,0:T(8,128)(2,1)S(1)} %get-tuple-element.47), channel_id=1, source_target_pairs={{0,13},{1,14},{2,15},{3,0},{4,1},{5,2},{6,3},{7,4},{8,5},{9,6},{10... | collective-permute-start | bytes 294920 | tf_op jit(solution)/shard_map/ppermute | solution.py:470
  38.2 10.1 %collective-permute-start.10 = (bf16[2,64,384]{2,1,0:T(8,128)(2,1)S(1)}, bf16[2,64,384]{2,1,0:T(8,128)(2,1)S(1)}, u32[]{:S(2)}, u32[]{:S(2)}) collective-permute-start(bf16[2,64,384]{2,1,0:T(8,128)(2,1)S(1)} %get-tuple-element.48), channel_id=1, source_target_pairs={{0,5},{1,6},{2,7},{3,8},{4,9},{5,10},{6,11},{7,12},{8,13},{9,14},{... | collective-permute-start | bytes 294920 | tf_op jit(solution)/shard_map/ppermute | solution.py:470
  38.2 10.1 %collective-permute-start.11 = (bf16[2,64,384]{2,1,0:T(8,128)(2,1)S(1)}, bf16[2,64,384]{2,1,0:T(8,128)(2,1)S(1)}, u32[]{:S(2)}, u32[]{:S(2)}) collective-permute-start(bf16[2,64,384]{2,1,0:T(8,128)(2,1)S(1)} %get-tuple-element.49), channel_id=1, source_target_pairs={{0,3},{1,4},{2,5},{3,6},{4,7},{5,8},{6,9},{7,10},{8,11},{9,12},{10... | collective-permute-start | bytes 294920 | tf_op jit(solution)/shard_map/ppermute | solution.py:470
  38.4 15.0 %collective-permute-start.12 = (bf16[2,64,384]{2,1,0:T(8,128)(2,1)S(1)}, bf16[2,64,384]{2,1,0:T(8,128)(2,1)S(1)}, u32[]{:S(2)}, u32[]{:S(2)}) collective-permute-start(bf16[2,64,384]{2,1,0:T(8,128)(2,1)S(1)} %get-tuple-element.50), channel_id=1, source_target_pairs={{0,11},{1,12},{2,13},{3,14},{4,15},{5,0},{6,1},{7,2},{8,3},{9,4},{... | collective-permute-start | bytes 294920 | tf_op jit(solution)/shard_map/ppermute | solution.py:470
  46.8 8.5 %collective-permute-start.13 = (bf16[2,64,384]{2,1,0:T(8,128)(2,1)S(1)}, bf16[2,64,384]{2,1,0:T(8,128)(2,1)S(1)}, u32[]{:S(2)}, u32[]{:S(2)}) collective-permute-start(bf16[2,64,384]{2,1,0:T(8,128)(2,1)S(1)} %get-tuple-element.51), channel_id=1, source_target_pairs={{0,12},{1,13},{2,14},{3,15},{4,0},{5,1},{6,2},{7,3},{8,4},{9,5},{1... | collective-permute-start | bytes 294920 | tf_op jit(solution)/shard_map/ppermute | solution.py:470
  47.4 8.0 %collective-permute-start.14 = (bf16[2,64,384]{2,1,0:T(8,128)(2,1)S(1)}, bf16[2,64,384]{2,1,0:T(8,128)(2,1)S(1)}, u32[]{:S(2)}, u32[]{:S(2)}) collective-permute-start(bf16[2,64,384]{2,1,0:T(8,128)(2,1)S(1)} %get-tuple-element.52), channel_id=1, source_target_pairs={{0,4},{1,5},{2,6},{3,7},{4,8},{5,9},{6,10},{7,11},{8,12},{9,13},{1... | collective-permute-start | bytes 294920 | tf_op jit(solution)/shard_map/ppermute | solution.py:470
  55.3 0.9 %copy-start.1 = (bf16[8,32,384]{2,1,0:T(8,128)(2,1)S(1)}, bf16[8,32,384]{2,1,0:T(8,128)(2,1)}, u32[]{:S(2)}) copy-start(bf16[8,32,384]{2,1,0:T(8,128)(2,1)} %ref.3) | copy-start | bytes 589828
  58.3 7.1 %collective-permute-start.15 = (bf16[8,16,384]{2,1,0:T(8,128)(2,1)S(1)}, bf16[8,16,384]{2,1,0:T(8,128)(2,1)S(1)}, u32[]{:S(2)}, u32[]{:S(2)}) collective-permute-start(bf16[8,16,384]{2,1,0:T(8,128)(2,1)S(1)} %get-tuple-element.54), channel_id=1, source_target_pairs={{1,2},{3,4},{5,6},{7,8},{9,10},{11,12},{13,14},{2,1},{4,3},{6,5},{... | collective-permute-start | bytes 294920 | tf_op jit(solution)/shard_map/ppermute | solution.py:22
  62.0 3.3 %collective-permute-start.16 = (bf16[8,16,384]{2,1,0:T(8,128)(2,1)S(1)}, bf16[8,16,384]{2,1,0:T(8,128)(2,1)S(1)}, u32[]{:S(2)}, u32[]{:S(2)}) collective-permute-start(bf16[8,16,384]{2,1,0:T(8,128)(2,1)S(1)} %get-tuple-element.55), channel_id=1, source_target_pairs={{0,1},{2,3},{4,5},{6,7},{8,9},{10,11},{12,13},{14,15},{1,0},{3,2},... | collective-permute-start | bytes 294920 | tf_op jit(solution)/shard_map/ppermute | solution.py:22
  (2 other events, 1.3 us)

commit v2 on v0

--- a/solution.py
+++ b/solution.py
@@ -38,7 +38,7 @@
     return owners, ranks, tiles
 
 
-def request_kernel(tiles_dev, pair_lists, table):
+def request_kernel(tiles_dev, pair_lists, _, table):
     n_view = table.shape[0]
     row = lax.broadcasted_iota(jnp.int32, (n_view, LANES), 0) * tiles_dev
     lane = lax.broadcasted_iota(jnp.int32, (n_view, LANES), 1)
@@ -89,30 +89,23 @@
     two_edge,
     bias_rows,
     bias_two,
-    scalars,
+    numbers,
     stacked_mid,
     stacked_edge,
 ):
     planes, sources = disparities.shape
     owners, ranks, _ = request_places(pair_lists, tiles_dev)
-    at = 0
-    for p in range(planes):
-        for s in range(sources):
-            scalars[at] = disparities[p, s]
-            at += 1
+    values = [disparities[p, s] for p in range(planes) for s in range(sources)]
     for owner, rank in zip(owners, ranks):
         back = lax.rem(me[0] - owner + n_view, n_view)
-        scalars[at] = jnp.where(owner >= 0, back * CAP + rank, 0)
-        at += 1
-    scalars[at] = view_counts[0]
-    scalars[at + 1] = me[0]
-    scalars[at + 2] = lax.rem(me[0], 2)
-    tail = kernel_edge.shape[0] - 8
+        values.append(jnp.where(owner >= 0, back * CAP + rank, 0))
+    values += [view_counts[0], me[0], lax.rem(me[0], 2)]
     lane_at = lax.broadcasted_iota(jnp.int32, (8, LANES), 1)
-    numbers = jnp.zeros((8, LANES), jnp.float32)
-    for i in range(at + 3):
-        numbers = jnp.where(lane_at == i, scalars[i].astype(jnp.float32), numbers)
-    kernel_edge[tail:, :] = numbers
+    row = jnp.zeros((8, LANES), jnp.int32)
+    for i, value in enumerate(values):
+        row = jnp.where(lane_at == i, value, row)
+    for at in range(0, numbers.shape[0], 8):
+        numbers[at : at + 8, :] = row
 
     c1, channels = first.shape[3], first.shape[4]
     c2 = second.shape[4]
@@ -253,26 +246,29 @@
     return result[:, :out_w]
 
 
-def edge_kernel(
-    at_slots, at_live, sources, blocks, picks, packed, arrived, ref, var, own, far, near, flags, wide, ref_wide, sums, held, sem
-):
+def warp_kernel(at_slots, at_live, sources, blocks, picks, numbers, arrived, ref, var, flags, wide, ref_wide, held, sem):
+    copy = pltpu.make_async_copy(numbers.at[pl.ds(0, 1)], held, sem)
+    copy.start()
     planes, cols, _ = var.shape
-    tail = packed.shape[0] - 8
-    c1 = tail // 27
-    copy = pltpu.make_async_copy(packed.at[pl.ds(tail, 1)], held, sem)
-    copy.start()
-    weights = packed[:tail].astype(jnp.bfloat16)
     turned = turned_reference(ref, blocks, picks)
     clear_bands(wide, cols)
     copy.wait()
-    scalars = [held[0, i].astype(jnp.int32) for i in range(at_live + 3)]
+    scalars = [held[0, i] for i in range(at_live + 3)]
     live = scalars[at_live]
     inv, scale = view_weights(live)
     ref_wide[0] = turned * scale
     load_tiles(at_slots, live, sources, blocks, picks, scale, scalars, arrived, wide)
-    odd = scalars[at_live + 2] > 0
-    flags[0] = jnp.where(odd, 1.0, 0.0) * jnp.ones((c1, LANES), jnp.float32)
-    flags[1] = jnp.where(scalars[at_live + 1] > 0, 1.0, 0.0) * jnp.ones((c1, LANES), jnp.float32)
+    flags[0] = jnp.where(scalars[at_live + 2] > 0, 1.0, 0.0) * jnp.ones(flags.shape[1:], jnp.float32)
+    flags[1] = jnp.where(scalars[at_live + 1] > 0, 1.0, 0.0) * jnp.ones(flags.shape[1:], jnp.float32)
+    for p in range(planes):
+        var[p] = plane_variance(p, sources, cols, scalars, wide, ref_wide, inv)
+
+
+def edge_kernel(var, kernel, flags, own, far, near, sums):
+    planes, cols, _ = var.shape
+    c1 = kernel.shape[0] // 27
+    odd = jnp.concatenate([jnp.concatenate([flags[0]] * 2, axis=0)] * (cols // LANES), axis=1) > 0.5
+    weights = kernel[...].astype(jnp.bfloat16)
     column = lax.broadcasted_iota(jnp.int32, (3 * c1, cols), 1)
     empty = jnp.zeros((c1, cols), jnp.float32)
 
@@ -284,13 +280,8 @@
         far[p] = jnp.where(odd, downward, upward).astype(jnp.bfloat16)
         near[p] = jnp.where(odd, upward, downward).astype(jnp.bfloat16)
 
-    values = plane_variance(0, sources, cols, scalars, wide, ref_wide, inv)
     for q in range(planes):
-        held_values = values
-        if q + 1 < planes:
-            values = plane_variance(q + 1, sources, cols, scalars, wide, ref_wide, inv)
-        add_plane(q, planes, held_values, weights, sums)
-        var[q] = held_values
+        add_plane(q, planes, var[q], weights, sums)
         if q > 0:
             finish(q - 1)
     finish(planes - 1)
@@ -317,10 +308,10 @@
     ref_wide,
     cost,
     sums,
-    scalars,
+    held,
     sem,
 ):
-    copy = pltpu.make_async_copy(numbers, scalars, sem)
+    copy = pltpu.make_async_copy(numbers.at[pl.ds(0, 1)], held, sem)
     copy.start()
     planes, cols, _ = edge_var.shape
     inner = cost.shape[0] // planes
@@ -332,6 +323,7 @@
     turned = turned_reference(ref, blocks, picks)
     clear_bands(wide, cols)
     copy.wait()
+    scalars = [held[0, i] for i in range(at_live + 1)]
     live = scalars[at_live]
     inv, scale = view_weights(live)
     ref_wide[0] = turned * scale
@@ -407,16 +399,16 @@
     bf16, f32, i32 = jnp.bfloat16, jnp.float32, jnp.int32
     shape = jax.ShapeDtypeStruct
 
+    tiles = source_tiles.reshape(tiles_dev, slab, cols)
     table = pl.pallas_call(
         functools.partial(request_kernel, tiles_dev),
         out_shape=shape((n_view, 1, 2 * CAP), i32),
-        in_specs=[vmem],
+        in_specs=[vmem, vmem],
         out_specs=vmem,
         compiler_params=params,
         name="request_table",
-    )(pair_lists)
+    )(pair_lists, tiles)
     table = lax.all_to_all(table, "view", split_axis=0, concat_axis=0, tiled=True)
-    tiles = source_tiles.reshape(tiles_dev, slab, cols)
     table = table[:, 0, : CAP + 1].reshape(1, n_view * (CAP + 1))
     far_first = sorted(range(1, n_view), key=lambda k: -min(k, n_view - k))
     order = [k for pair in zip(far_first, far_first[::-1]) for k in pair][: len(far_first)]
@@ -444,16 +436,16 @@
     prepared = pl.pallas_call(
         functools.partial(prepare_kernel, n_view, tiles_dev, edge_rows, mid_rows),
         out_shape=[
-            shape((27 * c1 + 8, LANES), f32),
+            shape((27 * c1, LANES), f32),
             shape((9 * (inner + c1), 2 * LANES), f32),
             shape((3 * half_r * c2, mid_deep), bf16),
             shape((3 * half_r * c2, edge_deep), bf16),
             shape((inner, cols), f32),
             shape((half_r * c2, half_x), f32),
-            shape((LANES,), i32),
+            shape((12 * 8, LANES), i32),
         ],
         in_specs=[vmem, vmem] + [smem] * 6,
-        out_specs=[vmem] * 6 + [smem],
+        out_specs=[vmem] * 7,
         scratch_shapes=[pltpu.VMEM((3 * mid_deep, LANES), f32), pltpu.VMEM((3 * edge_deep, LANES), f32)],
         compiler_params=params,
         name="weights_and_scalars",
@@ -467,7 +459,7 @@
         view_counts,
         me,
     )
-    kernel_edge, kernel_mid, two_mid, two_edge, bias_rows, bias_two, scalars = prepared
+    kernel_edge, kernel_mid, two_mid, two_edge, bias_rows, bias_two, numbers = prepared
     arrived = pl.pallas_call(
         functools.partial(collect_kernel, distances),
         out_shape=shape((n_view * CAP, slab, cols), bf16),
@@ -480,26 +472,24 @@
     band_scratch = [pltpu.VMEM((sources, cols + 2 * SHIFT, LANES), f32), pltpu.VMEM((1, cols, LANES), f32)]
     payload = shape((planes, 2 * c1, cols), bf16)
     col_step = (half_x // LANES + 1) * LANES
-    edge_var, own, far, near, flags = pl.pallas_call(
-        functools.partial(edge_kernel, at_slots, at_live, sources, blocks, edge_blocks),
-        out_shape=[
-            shape((planes, cols, LANES), bf16),
-            shape((planes, 2 * c1, cols), f32),
-            payload,
-            payload,
-            shape((2, c1, LANES), f32),
-        ],
+    edge_var, flags = pl.pallas_call(
+        functools.partial(warp_kernel, at_slots, at_live, sources, blocks, edge_blocks),
+        out_shape=[shape((planes, cols, LANES), bf16), shape((2, c1, LANES), f32)],
         in_specs=[vmem] * 3,
-        out_specs=[vmem] * 5,
-        scratch_shapes=band_scratch
-        + [
-            pltpu.VMEM((3, 9 * c1, cols), f32),
-            pltpu.SMEM((1, LANES), f32),
-            pltpu.SemaphoreType.DMA,
-        ],
+        out_specs=[vmem] * 2,
+        scratch_shapes=band_scratch + [pltpu.SMEM((1, LANES), i32), pltpu.SemaphoreType.DMA],
+        compiler_params=params,
+        name="edge_variance",
+    )(numbers, arrived, ref_features)
+    own, far, near = pl.pallas_call(
+        edge_kernel,
+        out_shape=[shape((planes, 2 * c1, cols), f32), payload, payload],
+        in_specs=[vmem] * 3,
+        out_specs=[vmem] * 3,
+        scratch_shapes=[pltpu.VMEM((3, 9 * c1, cols), f32)],
         compiler_params=params,
         name="edge_rows",
-    )(kernel_edge, arrived, ref_features)
+    )(edge_var, kernel_edge, flags)
     far = swapped(far, "view", 1)
     near = swapped(near, "view", 0)
 
@@ -510,18 +500,18 @@
             shape((planes, c1, cols), f32),
             shape((cols, 2 * col_step), bf16),
         ],
-        in_specs=[anywhere] + [vmem] * 7,
+        in_specs=[vmem] * 8,
         out_specs=[vmem] * 3,
         scratch_shapes=band_scratch
         + [
             pltpu.VMEM((planes * inner, cols), bf16),
             pltpu.VMEM((3, 3 * (inner + c1), cols), f32),
-            pltpu.SMEM(scalars.shape, i32),
+            pltpu.SMEM((1, LANES), i32),
             pltpu.SemaphoreType.DMA,
         ],
         compiler_params=params,
         name="middle_rows",
-    )(scalars, arrived, ref_features, edge_var, kernel_mid, bias_rows, two_mid, bias_two)
+    )(numbers, arrived, ref_features, edge_var, kernel_mid, bias_rows, two_mid, bias_two)
 
     out = pl.pallas_call(
         end_kernel,

time: 63.6 us -> 65.2 us (1.025)
  the two profiles are of different devices: /device:TPU:9 before, /device:TPU:0 now
where the time goes in v2:
time: 65.2 us; the launch traced here: 65 us
  starting transfers between devices  25.1 us (38%)
  blocking collectives  13.7 us (21%)
  waiting for transfers between devices  13.7 us (21%)
  Pallas kernels  8.55 us (13%)
  local copies, waits for them, and re-layouts  3.09 us (5%)
  between operations  0.84 us (1%)
    ppermute x15, starting transfers between devices, on_device(): bundles[k] = lax.ppermute(bundle, 'view', pairs) if k else bundle  20.9 us
    all_to_all x1, blocking collectives, on_device(): lax.all_to_all(table, 'view', split_axis=0, concat_axis=0, tiled=True)  13.7 us
    ppermute x15, waiting for transfers between devices, on_device(): bundles[k] = lax.ppermute(bundle, 'view', pairs) if k else bundle  13.7 us
    ppermute x2, starting transfers between devices, swapped(): return lax.ppermute(x, axis, pairs + [(j, i) for i, j in pairs])  4.19 us
    unnamed x21, local copies, waits for them, and re-layouts  2.98 us
    pallas_call x1, Pallas kernels, on_device(): pl.pallas_call(functools.partial(mid_kernel, at_slots, at_live, sources,...  2.92 us
    pallas_call x1, Pallas kernels, on_device(): pl.pallas_call(functools.partial(warp_kernel, at_slots, at_live, sources,...  1.64 us
  transfers between devices with their start and end apart: 17, of which 6 were waited for; matrix products, arithmetic and copies ran while one was open for 0% of the time, Pallas kernels for 6%

profile of v2, /device:TPU:0, one launch (start us, length us, event | category | flops | bytes accessed | tf_op | source)
XLA Modules:
  0.0 65.0 jit_solution(1467288181521639832)
XLA Ops:
  0.0 1.4 %copy-done = bf16[32,2,32,384]{3,2,1,0:T(8,128)(2,1)S(1)} copy-done((bf16[32,2,32,384]{3,2,1,0:T(8,128)(2,1)S(1)}, bf16[32,2,32,384]{3,2,1,0:T(8,128)(2,1)}, u32[]{:S(2)}) %copy-start) | copy-done | bytes 1572888
  1.4 0.7 %copy-done.5 = s32[1,4,4]{2,1,0:T(4,128)S(1)} copy-done((s32[1,4,4]{2,1,0:T(4,128)S(1)}, s32[1,4,4]{2,1,0:T(4,128)}, u32[]{:S(2)}) %copy-start.5) | copy-done | bytes 88
  2.3 13.7 %all_to_all.5 = s32[16,1,4]{2,1,0:T(1,128)S(1)} all-to-all(s32[16,1,4]{2,1,0:T(1,128)S(1)} %request_table.1), channel_id=1, replica_groups=mesh['groups'=2,'view'=16] {'view'}, dimensions={0} | all-to-all | bytes 512 | tf_op jit(solution)/shard_map/all_to_all | solution.py:411
  16.1 0.7 %requested_tiles.1 = (bf16[2,64,384]{2,1,0:T(8,128)(2,1)S(1)}, bf16[2,64,384]{2,1,0:T(8,128)(2,1)S(1)}, bf16[2,64,384]{2,1,0:T(8,128)(2,1)S(1)}, bf16[2,64,384]{...) custom-call(s32[1,48]{1,0:T(1,128)S(1)} %reshape_squeeze.3.table, ...), custom_call_target="tpu_custom_call" | custom-call | tf_op jit(solution)/shard_map/requested_tiles/pallas_call | solution.py:417
  17.4 1.5 %collective-permute-start.1 = (bf16[2,64,384]{2,1,0:T(8,128)(2,1)S(1)}, bf16[2,64,384]{2,1,0:T(8,128)(2,1)S(1)}, u32[]{:S(2)}, u32[]{:S(2)}) collective-permute-start(bf16[2,64,384]{2,1,0:T(8,128)(2,1)S(1)} %get-tuple-element.38), channel_id=1, source_target_pairs={{0,15},{1,0},{2,1},{3,2},{4,3},{5,4},{6,5},{7,6},{8,7},{9,8},{10,9... | collective-permute-start | bytes 294920 | tf_op jit(solution)/shard_map/ppermute | solution.py:427
  19.0 2.0 %collective-permute-start.11 = (bf16[2,64,384]{2,1,0:T(8,128)(2,1)S(1)}, bf16[2,64,384]{2,1,0:T(8,128)(2,1)S(1)}, u32[]{:S(2)}, u32[]{:S(2)}) collective-permute-start(bf16[2,64,384]{2,1,0:T(8,128)(2,1)S(1)} %get-tuple-element.48), channel_id=1, source_target_pairs={{0,3},{1,4},{2,5},{3,6},{4,7},{5,8},{6,9},{7,10},{8,11},{9,12},{10... | collective-permute-start | bytes 294920 | tf_op jit(solution)/shard_map/ppermute | solution.py:427
  21.0 1.5 %collective-permute-start.12 = (bf16[2,64,384]{2,1,0:T(8,128)(2,1)S(1)}, bf16[2,64,384]{2,1,0:T(8,128)(2,1)S(1)}, u32[]{:S(2)}, u32[]{:S(2)}) collective-permute-start(bf16[2,64,384]{2,1,0:T(8,128)(2,1)S(1)} %get-tuple-element.49), channel_id=1, source_target_pairs={{0,11},{1,12},{2,13},{3,14},{4,15},{5,0},{6,1},{7,2},{8,3},{9,4},{... | collective-permute-start | bytes 294920 | tf_op jit(solution)/shard_map/ppermute | solution.py:427
  22.5 6.3 %collective-permute-done.refs_0_ = bf16[2,64,384]{2,1,0:T(8,128)(2,1)S(1)} collective-permute-done((bf16[2,64,384]{2,1,0:T(8,128)(2,1)S(1)}, bf16[2,64,384]{2,1,0:T(8,128)(2,1)S(1)}, u32[]{:S(2)}, u32[]{:S(2)}) %collective-permute-start) | collective-permute-done | bytes 98336 | tf_op jit(solution)/shard_map/ppermute | solution.py:427
  28.8 2.0 %collective-permute-start.14 = (bf16[2,64,384]{2,1,0:T(8,128)(2,1)S(1)}, bf16[2,64,384]{2,1,0:T(8,128)(2,1)S(1)}, u32[]{:S(2)}, u32[]{:S(2)}) collective-permute-start(bf16[2,64,384]{2,1,0:T(8,128)(2,1)S(1)} %get-tuple-element.51), channel_id=1, source_target_pairs={{0,4},{1,5},{2,6},{3,7},{4,8},{5,9},{6,10},{7,11},{8,12},{9,13},{1... | collective-permute-start | bytes 294920 | tf_op jit(solution)/shard_map/ppermute | solution.py:427
  30.8 1.0 %collective-permute-start.2 = (bf16[2,64,384]{2,1,0:T(8,128)(2,1)S(1)}, bf16[2,64,384]{2,1,0:T(8,128)(2,1)S(1)}, u32[]{:S(2)}, u32[]{:S(2)}) collective-permute-start(bf16[2,64,384]{2,1,0:T(8,128)(2,1)S(1)} %get-tuple-element.39), channel_id=1, source_target_pairs={{0,7},{1,8},{2,9},{3,10},{4,11},{5,12},{6,13},{7,14},{8,15},{9,0},... | collective-permute-start | bytes 294920 | tf_op jit(solution)/shard_map/ppermute | solution.py:427
  31.8 2.1 %collective-permute-start.4 = (bf16[2,64,384]{2,1,0:T(8,128)(2,1)S(1)}, bf16[2,64,384]{2,1,0:T(8,128)(2,1)S(1)}, u32[]{:S(2)}, u32[]{:S(2)}) collective-permute-start(bf16[2,64,384]{2,1,0:T(8,128)(2,1)S(1)} %get-tuple-element.41), channel_id=1, source_target_pairs={{0,9},{1,10},{2,11},{3,12},{4,13},{5,14},{6,15},{7,0},{8,1},{9,2},... | collective-permute-start | bytes 294920 | tf_op jit(solution)/shard_map/ppermute | solution.py:427
  33.9 2.5 %collective-permute-done.13.refs_13_ = bf16[2,64,384]{2,1,0:T(8,128)(2,1)S(1)} collective-permute-done((bf16[2,64,384]{2,1,0:T(8,128)(2,1)S(1)}, bf16[2,64,384]{2,1,0:T(8,128)(2,1)S(1)}, u32[]{:S(2)}, u32[]{:S(2)}) %collective-permute-start.13) | collective-permute-done | bytes 98336 | tf_op jit(solution)/shard_map/ppermute | solution.py:427
  36.4 6.6 %collective-permute-start.6 = (bf16[2,64,384]{2,1,0:T(8,128)(2,1)S(1)}, bf16[2,64,384]{2,1,0:T(8,128)(2,1)S(1)}, u32[]{:S(2)}, u32[]{:S(2)}) collective-permute-start(bf16[2,64,384]{2,1,0:T(8,128)(2,1)S(1)} %get-tuple-element.43), channel_id=1, source_target_pairs={{0,6},{1,7},{2,8},{3,9},{4,10},{5,11},{6,12},{7,13},{8,14},{9,15},... | collective-permute-start | bytes 294920 | tf_op jit(solution)/shard_map/ppermute | solution.py:427
  43.0 1.7 %collective-permute-start.7 = (bf16[2,64,384]{2,1,0:T(8,128)(2,1)S(1)}, bf16[2,64,384]{2,1,0:T(8,128)(2,1)S(1)}, u32[]{:S(2)}, u32[]{:S(2)}) collective-permute-start(bf16[2,64,384]{2,1,0:T(8,128)(2,1)S(1)} %get-tuple-element.44), channel_id=1, source_target_pairs={{0,2},{1,3},{2,4},{3,5},{4,6},{5,7},{6,8},{7,9},{8,10},{9,11},{10,... | collective-permute-start | bytes 294920 | tf_op jit(solution)/shard_map/ppermute | solution.py:427
  44.7 1.6 %collective-permute-start.8 = (bf16[2,64,384]{2,1,0:T(8,128)(2,1)S(1)}, bf16[2,64,384]{2,1,0:T(8,128)(2,1)S(1)}, u32[]{:S(2)}, u32[]{:S(2)}) collective-permute-start(bf16[2,64,384]{2,1,0:T(8,128)(2,1)S(1)} %get-tuple-element.45), channel_id=1, source_target_pairs={{0,10},{1,11},{2,12},{3,13},{4,14},{5,15},{6,0},{7,1},{8,2},{9,3},... | collective-permute-start | bytes 294920 | tf_op jit(solution)/shard_map/ppermute | solution.py:427
  47.3 1.1 %weights_and_scalars.1 = (f32[216,128]{1,0:T(8,128)S(1)}, f32[504,256]{1,0:T(8,128)S(1)}, bf16[192,256]{1,0:T(8,128)(2,1)S(1)}, bf16[192,128]{1,0:T(8,128)(2,1)S...) custom-call(bf16[3,3,3,8,32]{4,3,2,1,0:T(8,128)(2,1)S(1)} %bitcast.7, ...), custom_call_target="tpu_custom_call" | custom-call | tf_op jit(solution)/shard_map/weights_and_scalars/pallas_call | solution.py:436
  49.1 1.7 %collective-permute-done.7.refs_7_ = bf16[2,64,384]{2,1,0:T(8,128)(2,1)S(1)} collective-permute-done((bf16[2,64,384]{2,1,0:T(8,128)(2,1)S(1)}, bf16[2,64,384]{2,1,0:T(8,128)(2,1)S(1)}, u32[]{:S(2)}, u32[]{:S(2)}) %collective-permute-start.7) | collective-permute-done | bytes 98336 | tf_op jit(solution)/shard_map/ppermute | solution.py:427
  50.8 1.7 %collective-permute-done.8.refs_8_ = bf16[2,64,384]{2,1,0:T(8,128)(2,1)S(1)} collective-permute-done((bf16[2,64,384]{2,1,0:T(8,128)(2,1)S(1)}, bf16[2,64,384]{2,1,0:T(8,128)(2,1)S(1)}, u32[]{:S(2)}, u32[]{:S(2)}) %collective-permute-start.8) | collective-permute-done | bytes 98336 | tf_op jit(solution)/shard_map/ppermute | solution.py:427
  52.5 0.9 %collective-permute-done.9.refs_9_ = bf16[2,64,384]{2,1,0:T(8,128)(2,1)S(1)} collective-permute-done((bf16[2,64,384]{2,1,0:T(8,128)(2,1)S(1)}, bf16[2,64,384]{2,1,0:T(8,128)(2,1)S(1)}, u32[]{:S(2)}, u32[]{:S(2)}) %collective-permute-start.9) | collective-permute-done | bytes 98336 | tf_op jit(solution)/shard_map/ppermute | solution.py:427
  53.5 0.8 %copy-done.2 = bf16[8,32,384]{2,1,0:T(8,128)(2,1)S(1)} copy-done((bf16[8,32,384]{2,1,0:T(8,128)(2,1)S(1)}, bf16[8,32,384]{2,1,0:T(8,128)(2,1)}, u32[]{:S(2)}) %copy-start.2) | copy-done | bytes 196632
  54.3 1.6 %edge_variance.1 = (bf16[8,384,128]{2,1,0:T(8,128)(2,1)S(1)}, f32[2,8,128]{2,1,0:T(8,128)S(1)}) custom-call(s32[96,128]{1,0:T(8,128)S(1)} %get-tuple-element.36.numbers, bf16[32,64,384]{2,1,0:T(8,128)(2,1)S(1)} %all_tiles.1.arrived, bf16[8,32,384]{2,1,0:T(8,128)(2,1)S(1)} %copy-done.2), custom_call_target="tpu_custom_call" | custom-call | tf_op jit(solution)/shard_map/edge_variance/pallas_call | solution.py:475
  57.3 3.5 %collective-permute-start.16 = (bf16[8,16,384]{2,1,0:T(8,128)(2,1)S(1)}, bf16[8,16,384]{2,1,0:T(8,128)(2,1)S(1)}, u32[]{:S(2)}, u32[]{:S(2)}) collective-permute-start(bf16[8,16,384]{2,1,0:T(8,128)(2,1)S(1)} %get-tuple-element.57), channel_id=1, source_target_pairs={{0,1},{2,3},{4,5},{6,7},{8,9},{10,11},{12,13},{14,15},{1,0},{3,2},... | collective-permute-start | bytes 294920 | tf_op jit(solution)/shard_map/ppermute | solution.py:22
  60.8 2.9 %middle_rows.1 = (f32[4,64,192]{2,1,0:T(8,128)S(1)}, f32[8,8,384]{2,1,0:T(8,128)S(1)}, bf16[384,512]{1,0:T(8,128)(2,1)S(1)}) custom-call(s32[96,128]{1,0:T(8,128)S(1)} %get-tuple-element.36.numbers, bf16[32,64,384]{2,1,0:T(8,128)(2,1)S(1)} %all_tiles.1.arrived, bf16[8,32,384]{2,1,0:T(8,128)(2,1)S(1)} %copy-done.2, ...), custom_call_target="tpu_custom_call" | custom-call | tf_op jit(solution)/shard_map/middle_rows/pallas_call | solution.py:496
  63.7 1.3 %end_rows.1 = f32[4,64,192]{2,1,0:T(8,128)} custom-call(bf16[8,16,384]{2,1,0:T(8,128)(2,1)S(1)} %collective-permute-done.15.far, bf16[8,16,384]{2,1,0:T(8,128)(2,1)S(1)} %collective-permute-done.16.near, f32[2,8,128]{2,1,0:T(8,128)S(1)} %get-tuple-element.55.flags, f32[8,16,384]{2,1,0:T(8,128)S(1)} %get-tuple-element.58.own, ...), custom_call_target="tpu_custom_call" | custom-call | tf_op jit(solution)/shard_map/end_rows/pallas_call | solution.py:516
  (42 shorter events, 3.3 us)
Async XLA Ops:
  2.1 14.0 %copy-start.1 = (bf16[32,2,32,384]{3,2,1,0:T(8,128)(2,1)S(1)}, bf16[32,2,32,384]{3,2,1,0:T(8,128)(2,1)}, u32[]{:S(2)}) copy-start(bf16[32,2,32,384]{3,2,1,0:T(8,128)(2,1)} %param.10) | copy-start | bytes 4718596
  2.1 44.5 %copy-start.9 = (s32[8,4]{0,1:T(4,128)S(1)}, s32[8,4]{0,1:T(4,128)}, u32[]{:S(2)}) copy-start(s32[8,4]{0,1:T(4,128)} %param.13) | copy-start | bytes 388
  2.1 45.2 %copy-start.3 = (bf16[3,3,8,3,32]{4,2,3,1,0:T(8,128)(2,1)S(1)}, bf16[3,3,8,3,32]{4,2,3,1,0:T(8,128)(2,1)}, u32[]{:S(2)}) copy-start(bf16[3,3,8,3,32]{4,2,3,1,0:T(8,128)(2,1)} %param.14) | copy-start | bytes 41476
  2.1 45.2 %copy-start.4 = (bf16[16,3,3,3,8]{0,4,3,2,1:T(8,128)(2,1)S(1)}, bf16[16,3,3,3,8]{0,4,3,2,1:T(8,128)(2,1)}, u32[]{:S(2)}) copy-start(bf16[16,3,3,3,8]{0,4,3,2,1:T(8,128)(2,1)} %param.16) | copy-start | bytes 20740
  2.1 45.2 %copy-start.6 = (s32[1,4,4]{2,1,0:T(4,128)S(1)}, s32[1,4,4]{2,1,0:T(4,128)}, u32[]{:S(2)}) copy-start(s32[1,4,4]{2,1,0:T(4,128)} %pair_lists.3) | copy-start | bytes 196
  2.1 45.2 %copy-start.7 = (f32[8]{0:T(128)S(1)}, f32[8]{0:T(128)}, u32[]{:S(2)}) copy-start(f32[8]{0:T(128)} %bias_first.1) | copy-start | bytes 100
  2.1 45.2 %copy-start.8 = (f32[16]{0:T(128)S(1)}, f32[16]{0:T(128)}, u32[]{:S(2)}) copy-start(f32[16]{0:T(128)} %bias_second.1) | copy-start | bytes 196
  16.9 11.9 %collective-permute-start = (bf16[2,64,384]{2,1,0:T(8,128)(2,1)S(1)}, bf16[2,64,384]{2,1,0:T(8,128)(2,1)S(1)}, u32[]{:S(2)}, u32[]{:S(2)}) collective-permute-start(bf16[2,64,384]{2,1,0:T(8,128)(2,1)S(1)} %get-tuple-element.37), channel_id=1, source_target_pairs={{0,8},{1,9},{2,10},{3,11},{4,12},{5,13},{6,14},{7,15},{8,0},{9,1},... | collective-permute-start | bytes 294920 | tf_op jit(solution)/shard_map/ppermute | solution.py:427
  17.4 11.3 %collective-permute-start.1 = (bf16[2,64,384]{2,1,0:T(8,128)(2,1)S(1)}, bf16[2,64,384]{2,1,0:T(8,128)(2,1)S(1)}, u32[]{:S(2)}, u32[]{:S(2)}) collective-permute-start(bf16[2,64,384]{2,1,0:T(8,128)(2,1)S(1)} %get-tuple-element.38), channel_id=1, source_target_pairs={{0,15},{1,0},{2,1},{3,2},{4,3},{5,4},{6,5},{7,6},{8,7},{9,8},{10,9... | collective-permute-start | bytes 294920 | tf_op jit(solution)/shard_map/ppermute | solution.py:427
  19.0 11.8 %collective-permute-start.10 = (bf16[2,64,384]{2,1,0:T(8,128)(2,1)S(1)}, bf16[2,64,384]{2,1,0:T(8,128)(2,1)S(1)}, u32[]{:S(2)}, u32[]{:S(2)}) collective-permute-start(bf16[2,64,384]{2,1,0:T(8,128)(2,1)S(1)} %get-tuple-element.47), channel_id=1, source_target_pairs={{0,5},{1,6},{2,7},{3,8},{4,9},{5,10},{6,11},{7,12},{8,13},{9,14},{... | collective-permute-start | bytes 294920 | tf_op jit(solution)/shard_map/ppermute | solution.py:427
  19.0 12.8 %collective-permute-start.11 = (bf16[2,64,384]{2,1,0:T(8,128)(2,1)S(1)}, bf16[2,64,384]{2,1,0:T(8,128)(2,1)S(1)}, u32[]{:S(2)}, u32[]{:S(2)}) collective-permute-start(bf16[2,64,384]{2,1,0:T(8,128)(2,1)S(1)} %get-tuple-element.48), channel_id=1, source_target_pairs={{0,3},{1,4},{2,5},{3,6},{4,7},{5,8},{6,9},{7,10},{8,11},{9,12},{10... | collective-permute-start | bytes 294920 | tf_op jit(solution)/shard_map/ppermute | solution.py:427
  21.0 10.8 %collective-permute-start.12 = (bf16[2,64,384]{2,1,0:T(8,128)(2,1)S(1)}, bf16[2,64,384]{2,1,0:T(8,128)(2,1)S(1)}, u32[]{:S(2)}, u32[]{:S(2)}) collective-permute-start(bf16[2,64,384]{2,1,0:T(8,128)(2,1)S(1)} %get-tuple-element.49), channel_id=1, source_target_pairs={{0,11},{1,12},{2,13},{3,14},{4,15},{5,0},{6,1},{7,2},{8,3},{9,4},{... | collective-permute-start | bytes 294920 | tf_op jit(solution)/shard_map/ppermute | solution.py:427
  28.8 7.6 %collective-permute-start.13 = (bf16[2,64,384]{2,1,0:T(8,128)(2,1)S(1)}, bf16[2,64,384]{2,1,0:T(8,128)(2,1)S(1)}, u32[]{:S(2)}, u32[]{:S(2)}) collective-permute-start(bf16[2,64,384]{2,1,0:T(8,128)(2,1)S(1)} %get-tuple-element.50), channel_id=1, source_target_pairs={{0,12},{1,13},{2,14},{3,15},{4,0},{5,1},{6,2},{7,3},{8,4},{9,5},{1... | collective-permute-start | bytes 294920 | tf_op jit(solution)/shard_map/ppermute | solution.py:427
  28.8 7.6 %collective-permute-start.14 = (bf16[2,64,384]{2,1,0:T(8,128)(2,1)S(1)}, bf16[2,64,384]{2,1,0:T(8,128)(2,1)S(1)}, u32[]{:S(2)}, u32[]{:S(2)}) collective-permute-start(bf16[2,64,384]{2,1,0:T(8,128)(2,1)S(1)} %get-tuple-element.51), channel_id=1, source_target_pairs={{0,4},{1,5},{2,6},{3,7},{4,8},{5,9},{6,10},{7,11},{8,12},{9,13},{1... | collective-permute-start | bytes 294920 | tf_op jit(solution)/shard_map/ppermute | solution.py:427
  30.8 12.2 %collective-permute-start.2 = (bf16[2,64,384]{2,1,0:T(8,128)(2,1)S(1)}, bf16[2,64,384]{2,1,0:T(8,128)(2,1)S(1)}, u32[]{:S(2)}, u32[]{:S(2)}) collective-permute-start(bf16[2,64,384]{2,1,0:T(8,128)(2,1)S(1)} %get-tuple-element.39), channel_id=1, source_target_pairs={{0,7},{1,8},{2,9},{3,10},{4,11},{5,12},{6,13},{7,14},{8,15},{9,0},... | collective-permute-start | bytes 294920 | tf_op jit(solution)/shard_map/ppermute | solution.py:427
  31.8 12.9 %collective-permute-start.3 = (bf16[2,64,384]{2,1,0:T(8,128)(2,1)S(1)}, bf16[2,64,384]{2,1,0:T(8,128)(2,1)S(1)}, u32[]{:S(2)}, u32[]{:S(2)}) collective-permute-start(bf16[2,64,384]{2,1,0:T(8,128)(2,1)S(1)} %get-tuple-element.40), channel_id=1, source_target_pairs={{0,1},{1,2},{2,3},{3,4},{4,5},{5,6},{6,7},{7,8},{8,9},{9,10},{10,1... | collective-permute-start | bytes 294920 | tf_op jit(solution)/shard_map/ppermute | solution.py:427
  31.8 14.5 %collective-permute-start.4 = (bf16[2,64,384]{2,1,0:T(8,128)(2,1)S(1)}, bf16[2,64,384]{2,1,0:T(8,128)(2,1)S(1)}, u32[]{:S(2)}, u32[]{:S(2)}) collective-permute-start(bf16[2,64,384]{2,1,0:T(8,128)(2,1)S(1)} %get-tuple-element.41), channel_id=1, source_target_pairs={{0,9},{1,10},{2,11},{3,12},{4,13},{5,14},{6,15},{7,0},{8,1},{9,2},... | collective-permute-start | bytes 294920 | tf_op jit(solution)/shard_map/ppermute | solution.py:427
  36.3 12.1 %collective-permute-start.5 = (bf16[2,64,384]{2,1,0:T(8,128)(2,1)S(1)}, bf16[2,64,384]{2,1,0:T(8,128)(2,1)S(1)}, u32[]{:S(2)}, u32[]{:S(2)}) collective-permute-start(bf16[2,64,384]{2,1,0:T(8,128)(2,1)S(1)} %get-tuple-element.42), channel_id=1, source_target_pairs={{0,14},{1,15},{2,0},{3,1},{4,2},{5,3},{6,4},{7,5},{8,6},{9,7},{10,... | collective-permute-start | bytes 294920 | tf_op jit(solution)/shard_map/ppermute | solution.py:427
  36.4 12.7 %collective-permute-start.6 = (bf16[2,64,384]{2,1,0:T(8,128)(2,1)S(1)}, bf16[2,64,384]{2,1,0:T(8,128)(2,1)S(1)}, u32[]{:S(2)}, u32[]{:S(2)}) collective-permute-start(bf16[2,64,384]{2,1,0:T(8,128)(2,1)S(1)} %get-tuple-element.43), channel_id=1, source_target_pairs={{0,6},{1,7},{2,8},{3,9},{4,10},{5,11},{6,12},{7,13},{8,14},{9,15},... | collective-permute-start | bytes 294920 | tf_op jit(solution)/shard_map/ppermute | solution.py:427
  43.0 7.8 %collective-permute-start.7 = (bf16[2,64,384]{2,1,0:T(8,128)(2,1)S(1)}, bf16[2,64,384]{2,1,0:T(8,128)(2,1)S(1)}, u32[]{:S(2)}, u32[]{:S(2)}) collective-permute-start(bf16[2,64,384]{2,1,0:T(8,128)(2,1)S(1)} %get-tuple-element.44), channel_id=1, source_target_pairs={{0,2},{1,3},{2,4},{3,5},{4,6},{5,7},{6,8},{7,9},{8,10},{9,11},{10,... | collective-permute-start | bytes 294920 | tf_op jit(solution)/shard_map/ppermute | solution.py:427
  44.7 7.8 %collective-permute-start.8 = (bf16[2,64,384]{2,1,0:T(8,128)(2,1)S(1)}, bf16[2,64,384]{2,1,0:T(8,128)(2,1)S(1)}, u32[]{:S(2)}, u32[]{:S(2)}) collective-permute-start(bf16[2,64,384]{2,1,0:T(8,128)(2,1)S(1)} %get-tuple-element.45), channel_id=1, source_target_pairs={{0,10},{1,11},{2,12},{3,13},{4,14},{5,15},{6,0},{7,1},{8,2},{9,3},... | collective-permute-start | bytes 294920 | tf_op jit(solution)/shard_map/ppermute | solution.py:427
  46.3 7.1 %collective-permute-start.9 = (bf16[2,64,384]{2,1,0:T(8,128)(2,1)S(1)}, bf16[2,64,384]{2,1,0:T(8,128)(2,1)S(1)}, u32[]{:S(2)}, u32[]{:S(2)}) collective-permute-start(bf16[2,64,384]{2,1,0:T(8,128)(2,1)S(1)} %get-tuple-element.46), channel_id=1, source_target_pairs={{0,13},{1,14},{2,15},{3,0},{4,1},{5,2},{6,3},{7,4},{8,5},{9,6},{10... | collective-permute-start | bytes 294920 | tf_op jit(solution)/shard_map/ppermute | solution.py:427
  56.6 7.1 %collective-permute-start.15 = (bf16[8,16,384]{2,1,0:T(8,128)(2,1)S(1)}, bf16[8,16,384]{2,1,0:T(8,128)(2,1)S(1)}, u32[]{:S(2)}, u32[]{:S(2)}) collective-permute-start(bf16[8,16,384]{2,1,0:T(8,128)(2,1)S(1)} %get-tuple-element.56), channel_id=1, source_target_pairs={{1,2},{3,4},{5,6},{7,8},{9,10},{11,12},{13,14},{2,1},{4,3},{6,5},{... | collective-permute-start | bytes 294920 | tf_op jit(solution)/shard_map/ppermute | solution.py:22
  57.3 6.5 %collective-permute-start.16 = (bf16[8,16,384]{2,1,0:T(8,128)(2,1)S(1)}, bf16[8,16,384]{2,1,0:T(8,128)(2,1)S(1)}, u32[]{:S(2)}, u32[]{:S(2)}) collective-permute-start(bf16[8,16,384]{2,1,0:T(8,128)(2,1)S(1)} %get-tuple-element.57), channel_id=1, source_target_pairs={{0,1},{2,3},{4,5},{6,7},{8,9},{10,11},{12,13},{14,15},{1,0},{3,2},... | collective-permute-start | bytes 294920 | tf_op jit(solution)/shard_map/ppermute | solution.py:22
  (3 other events, 3.0 us)
